TPU v7x, 32 devices: a whole 2x2x4 slice. The times are simulated.
32 devices in a mesh: rep: 2 (over y), row: 4 (over z), col: 4 (over x, core).
Axes of the slice: x: 2, y: 2, z: 4, core: 2. Of those that a mesh axis runs over, the one named last changes fastest.
Arguments:
- hidden_in: bfloat16 [8, 16384], P('rep', 'row'), parts along dimension 0, may hold values from -6 to 6
- norm_gain: float32 [16384], P('row'), may hold values from 0.5 to 1.5
- w_query: bfloat16 [16384, 8192], P('row', 'col'), may hold values from -0.046875 to 0.046875
- key_weight: bfloat16 [16384, 512], P('row', 'col'), may hold values from -0.046875 to 0.046875
- value_weight: bfloat16 [16384, 512], P('row', 'col'), may hold values from -0.046875 to 0.046875
- w_output: bfloat16 [8192, 16384], P('col', 'row'), may hold values from -3 to 3
- stored_keys: bfloat16 [8, 2048, 512], P(('rep', 'row'), None, 'col'), parts along dimension 0, may hold values from -480 to 480
- stored_values: bfloat16 [8, 2048, 512], P(('rep', 'row'), None, 'col'), parts along dimension 0, may hold values from -6 to 6
- lengths: int32 [8], P(('rep', 'row')), parts along dimension 0, may hold values from 256 to 2048, as said below
Outputs:
- attn_out: bfloat16 [8, 16384], P(('rep', 'col'), 'row'), parts along dimension 0
There are 2 independent parts, one for each index of `rep`. A program takes and returns all parts, laid end to end along the dimension named above; an argument that names none is the same for every part. Nothing has to cross between parts.
Inputs may be any that keep to these rules, and one draw needn't show every extreme that they name: `lengths`: each length is at least 256 and at most 2048; some request has exactly 2048.
All inputs are finite; a program needn't handle non-finite values.
Results may differ from a plain program's by a relative error of at most 0.0055.
The roundings to bfloat16 on the way count: a program that leaves them out, or rounds other values in their place, can miss the bound.
Values may be sent and summed in bfloat16 or wider, within the bound.
No kernel may reach another device: no remote copies, remote signals or barrier semaphores. Data moves between devices by JAX's collectives and lax.ppermute only.
A program may use at most 128 MiB of HBM per device.

v0:
```python
import jax
import jax.numpy as jnp
from jax import lax
from jax.sharding import PartitionSpec as P

MODEL_WIDTH = 16384
QUERY_HEADS = 64
KEY_VALUE_HEADS = 4
HEAD_WIDTH = 128


def apply_rotation(values, positions):
    half_dim = values.shape[-1] // 2
    head_size = values.shape[-1]
    frequency = 500000.0 ** (-(jnp.arange(half_dim, dtype=jnp.float32) * 2.0 / head_size))
    angles = positions.astype(jnp.float32)[:, None] * frequency[None, :]
    cosine = jnp.cos(angles)[:, None, :]
    sine_part = jnp.sin(angles)[:, None, :]
    first = values[..., :half_dim]
    second = values[..., half_dim:]
    return jnp.concatenate(
        [first * cosine - second * sine_part, second * cosine + first * sine_part], axis=-1
    )


def body(
    hidden_in,
    norm_gain,
    w_query,
    key_weight,
    value_weight,
    w_output,
    stored_keys,
    stored_values,
    lengths,
):
    per_device = stored_keys.shape[0]
    capacity = stored_keys.shape[1]
    group_size = QUERY_HEADS // KEY_VALUE_HEADS
    head_size = HEAD_WIDTH
    kv_heads = stored_keys.shape[2] // head_size
    query_width = w_query.shape[1]
    kv_width = key_weight.shape[1]
    inputs = hidden_in.astype(jnp.float32)
    sum_squares = lax.psum(jnp.sum(inputs * inputs, axis=1), "row")
    row_scale = lax.rsqrt(sum_squares / MODEL_WIDTH + 1e-05)
    normed = (inputs * norm_gain[None, :]).astype(jnp.bfloat16)
    first_row = lax.axis_index("row") * per_device
    my_scale = lax.dynamic_slice_in_dim(row_scale, first_row, per_device, 0)[:, None]
    weights_all = jnp.concatenate([w_query, key_weight, value_weight], axis=1)
    projected = lax.psum_scatter(
        jnp.dot(normed, weights_all, preferred_element_type=jnp.float32),
        "row",
        scatter_dimension=0,
        tiled=True,
    )
    query_part = projected[:, :query_width]
    key_part = projected[:, query_width : query_width + kv_width]
    value_part = projected[:, query_width + kv_width :]
    query_rotated_rows = apply_rotation(
        (query_part * my_scale).reshape(per_device, kv_heads * group_size, head_size), lengths
    )
    query_rotated_rows = query_rotated_rows.astype(jnp.bfloat16).reshape(
        per_device, kv_heads, group_size, head_size
    )
    key_rotated_rows = apply_rotation(
        (key_part * my_scale).reshape(per_device, kv_heads, head_size), lengths
    ).astype(jnp.bfloat16)
    value_request_rows = (
        (value_part * my_scale).reshape(per_device, kv_heads, head_size).astype(jnp.bfloat16)
    )
    every_key = stored_keys.reshape(per_device, capacity, kv_heads, head_size)
    every_value = stored_values.reshape(per_device, capacity, kv_heads, head_size)
    inverse = 1.0 / head_size**0.5
    score_new = (
        jnp.einsum(
            "rkgd,rkd->rkg",
            query_rotated_rows,
            key_rotated_rows,
            preferred_element_type=jnp.float32,
        )
        * inverse
    )
    tail_new = value_request_rows.astype(jnp.float32)[:, :, None, :]
    scores = (
        jnp.einsum(
            "rkgd,rckd->rkgc", query_rotated_rows, every_key, preferred_element_type=jnp.float32
        )
        * inverse
    )
    is_live = (jnp.arange(capacity, dtype=jnp.int32)[None, :] < lengths[:, None])[:, None, None, :]
    largest = jnp.maximum(jnp.max(jnp.where(is_live, scores, -jnp.inf), axis=-1), score_new)
    expo = jnp.where(is_live, jnp.exp(scores - largest[..., None]), 0.0)
    expo_new = jnp.exp(score_new - largest)
    denom = jnp.sum(expo, axis=-1) + expo_new
    probs = (expo / denom[..., None]).astype(jnp.bfloat16)
    prob_new = (expo_new / denom).astype(jnp.bfloat16)
    heads_out = jnp.einsum(
        "rkgc,rckd->rkgd", probs, every_value, preferred_element_type=jnp.float32
    )
    heads_out = heads_out + prob_new.astype(jnp.float32)[..., None] * tail_new
    heads_out = heads_out.astype(jnp.bfloat16).reshape(
        per_device, kv_heads * group_size * head_size
    )
    partial_out = jnp.dot(
        lax.all_gather(heads_out, "row", axis=0, tiled=True),
        w_output,
        preferred_element_type=jnp.float32,
    )
    return lax.psum_scatter(partial_out, "col", scatter_dimension=0, tiled=True).astype(
        jnp.bfloat16
    )


def solution(mesh):
    placed = (
        P("rep", "row"),
        P("row"),
        P("row", "col"),
        P("row", "col"),
        P("row", "col"),
        P("col", "row"),
        P(("rep", "row"), None, "col"),
        P(("rep", "row"), None, "col"),
        P(("rep", "row")),
    )
    return jax.shard_map(
        body, mesh=mesh, in_specs=placed, out_specs=P(("rep", "col"), "row"), check_vma=False
    )
```

profile of v0, /device:TPU:0, one launch (start us, length us, event | category | flops | bytes accessed | tf_op | source)
XLA Modules:
  0.0 70.8 jit_solution(17521413497115603581)
XLA Ops:
  0.0 0.0 copy-start
  0.7 1.2 %dynamic-slice.2 = u32[1]{0:T(128)} dynamic-slice(u32[32]{0:T(128)} %constant.38, u32[]{:T(128)S(6)} %add.33), dynamic_slice_sizes={1} | dynamic-slice | bytes 12
  2.0 1.3 %dynamic-slice = u32[1]{0:T(128)} dynamic-slice(u32[32]{0:T(128)} %constant.34, u32[]{:T(128)S(6)} %add.33), dynamic_slice_sizes={1} | dynamic-slice | bytes 12
  3.2 0.9 %fusion.12 = f32[4]{0:T(128)S(1)} fusion(bf16[4,4096]{1,0:T(4,128)(2,1)} %param.9), kind=kLoop, calls=%fused_computation.20 | loop fusion | flops 49148 | bytes 32784 | tf_op jit(solution)/shard_map/reduce_sum | solution.py:45
  4.2 0.0 copy-start.1
  4.2 7.9 %fusion = f32[4,2304]{1,0:T(4,128)S(1)} fusion(bf16[4096,128]{1,0:T(8,128)(2,1)} %param.13, bf16[4096,128]{1,0:T(8,128)(2,1)} %param.12, bf16[4096,2048]{1,0:T(8,128)(2,1)} %param.11, bf16[4,4096]{1,0:T(4,128)(2,1)} %param.9, f32[4096]{0:T(1024)} %param.10), kind=kOutput, calls=%fused_computation | convolution fusion | flops 132169728 | bytes 18960384 | tf_op jit(solution)/shard_map/dot_general | solution.py:52
  12.1 21.2 %all-reduce.2 = (f32[4,2304]{1,0:T(4,128)S(1)}, f32[4]{0:T(128)S(1)}) all-reduce(f32[4,2304]{1,0:T(4,128)S(1)} %fusion, f32[4]{0:T(128)S(1)} %fusion.12), channel_id=2, replica_groups=mesh['rep'=2,'row'=4,'col'=4] {'row'}, use_global_device_ids=true, to_apply=%region_0.0.clone | all-reduce | flops 9220 | bytes 73760
  33.3 0.6 dynamic_slice.3
  33.9 1.4 %fusion.26 = (f32[128]{0:T(128)S(1)}, f32[1,1,128]{2,1,0:T(1,128)S(1)}) fusion(f32[4,2304]{1,0:T(4,128)S(1)} %get-tuple-element.5, u32[]{:T(128)} %bitcast.14, u32[]{:T(128)S(6)} %convert.23, f32[]{:T(128)} %bitcast.1, u32[]{:T(128)S(6)} %convert.22), kind=kLoop, calls=%fused_computation.40 | loop fusion | flops 512 | bytes 2064 | tf_op jit(solution)/shard_map/convert_element_type | solution.py:84
  35.3 1.3 %dynamic-slice_multiply_fusion = f32[1,2048]{1,0:T(1,128)S(1)} fusion(f32[4,2304]{1,0:T(4,128)S(1)} %get-tuple-element.5, u32[]{:T(128)} %bitcast.14, f32[]{:T(128)} %bitcast.1), kind=kLoop, calls=%fused_computation.30 | loop fusion | flops 2048 | bytes 16392 | tf_op jit(solution)/shard_map/mul | solution.py:61
  36.5 0.1 fusion.22
  36.6 0.1 convert_bitcast_fusion.1
  36.7 0.0 copy-done
  36.7 0.4 select_reduce_fusion
  37.1 0.2 fusion.39
  37.3 0.2 fusion.10
  37.5 0.0 copy-done.1
  37.5 0.3 fusion.6
  37.8 13.1 %all-gather = bf16[4,1,2048]{2,1,0:T(2,128)(2,1)S(1)} all-gather(bf16[1,1,2048]{2,1,0:T(2,128)(2,1)S(1)} %reshape.176), channel_id=1, replica_groups=mesh['rep'=2,'row'=4,'col'=4] {'row'}, dimensions={0}, use_global_device_ids=true | all-gather | bytes 20480 | tf_op jit(solution)/shard_map/all_gather | solution.py:106
  50.9 8.0 %fusion.19 = f32[4,4096]{1,0:T(4,128)S(1)} fusion(bf16[2048,4096]{1,0:T(8,128)(2,1)} %param.14, bf16[4,1,2048]{2,1,0:T(2,128)(2,1)S(1)} %all-gather), kind=kOutput, calls=%fused_computation.26 | convolution fusion | flops 67108864 | bytes 16859136 | tf_op jit(solution)/shard_map/dot_general | solution.py:105
  59.0 10.7 %all-reduce.1 = bf16[4,4096]{1,0:T(4,128)(2,1)S(1)} all-reduce(f32[4,4096]{1,0:T(4,128)S(1)} %fusion.19), channel_id=3, replica_groups=mesh['rep'=2,'row'=4,'col'=4] {'col'}, use_global_device_ids=true, to_apply=%region_5.6.clone | all-reduce | flops 16384 | bytes 98304
  69.6 1.2 %dynamic-slice_convert_fusion = bf16[1,4096]{1,0:T(2,128)(2,1)} fusion(bf16[4,4096]{1,0:T(4,128)(2,1)S(1)} %all-reduce.1, u32[]{:T(128)} %bitcast.16), kind=kLoop, calls=%fused_computation.29 | loop fusion | bytes 16388 | tf_op jit(solution)/shard_map/convert_element_type | solution.py:110
  (5 shorter events, 0.1 us)
Async XLA Ops:
  0.0 36.7 %copy-start = (bf16[1,2048,128]{2,1,0:T(8,128)(2,1)S(1)}, bf16[1,2048,128]{2,1,0:T(8,128)(2,1)}, u32[]{:S(2)}) copy-start(bf16[1,2048,128]{2,1,0:T(8,128)(2,1)} %param.15) | copy-start | bytes 1572868
  4.2 33.4 %copy-start.1 = (bf16[1,2048,128]{2,1,0:T(8,128)(2,1)S(1)}, bf16[1,2048,128]{2,1,0:T(8,128)(2,1)}, u32[]{:S(2)}) copy-start(bf16[1,2048,128]{2,1,0:T(8,128)(2,1)} %param.16) | copy-start | bytes 1572868
where the time goes:
time: 71.2 us; the launch traced here: 70.8 us
  blocking collectives  45 us (63%)
  matrix products  16.8 us (24%)
  local copies, waits for them, and re-layouts  4.3 us (6%)
  other arithmetic  3.99 us (6%)
  between operations  0.79 us (1%)
    unnamed x2, blocking collectives  31.9 us
    all_gather x1, blocking collectives, body(): lax.all_gather(heads_out, 'row', axis=0, tiled=True)  13.1 us
    dot_general x1, matrix products, body(): jnp.dot(lax.all_gather(heads_out, 'row', axis=0, tiled=True), w_output, p...  8.04 us
    dot_general x1, matrix products, body(): jnp.dot(normed, weights_all, preferred_element_type=jnp.float32)  7.86 us
    unnamed x7, local copies, waits for them, and re-layouts  2.52 us

commit v1 on v0

--- a/solution.py
+++ b/solution.py
@@ -1,3 +1,5 @@
+import functools
+
 import jax
 import jax.numpy as jnp
 from jax import lax
@@ -23,7 +25,57 @@
     )
 
 
+DIRECT_LIMIT = 8
+
+
+def is_direct(size):
+    return 1 < size <= DIRECT_LIMIT and size & (size - 1) == 0
+
+
+def partner_order(size):
+    return range(size - 1, 0, -1)
+
+
+def swap_with(values, axis, size, mask):
+    return lax.ppermute(values, axis, [(i, i ^ mask) for i in range(size)])
+
+
+def scatter_sum(values, axis, size):
+    if not is_direct(size):
+        return lax.psum_scatter(values, axis, scatter_dimension=0, tiled=True)
+    share = values.shape[0] // size
+    me = lax.axis_index(axis)
+    total = lax.dynamic_slice_in_dim(values, me * share, share, 0)
+    received = [
+        swap_with(
+            lax.dynamic_slice_in_dim(values, (me ^ mask) * share, share, 0), axis, size, mask
+        )
+        for mask in partner_order(size)
+    ]
+    for part in received:
+        total = total + part
+    return total
+
+
+def gather_rows(values, axis, size):
+    if not is_direct(size):
+        return lax.all_gather(values, axis, axis=0, tiled=True)
+    me = lax.axis_index(axis)
+    blocks = [values] * size
+    for mask in partner_order(size):
+        blocks[mask] = swap_with(values, axis, size, mask)
+    ordered = []
+    for place in range(size):
+        block = blocks[0]
+        for mask in range(1, size):
+            block = jnp.where((me ^ mask) == place, blocks[mask], block)
+        ordered.append(block)
+    return jnp.concatenate(ordered, axis=0)
+
+
 def body(
+    row_size,
+    col_size,
     hidden_in,
     norm_gain,
     w_query,
@@ -42,21 +94,16 @@
     query_width = w_query.shape[1]
     kv_width = key_weight.shape[1]
     inputs = hidden_in.astype(jnp.float32)
-    sum_squares = lax.psum(jnp.sum(inputs * inputs, axis=1), "row")
-    row_scale = lax.rsqrt(sum_squares / MODEL_WIDTH + 1e-05)
+    squares = jnp.sum(inputs * inputs, axis=1, keepdims=True)
     normed = (inputs * norm_gain[None, :]).astype(jnp.bfloat16)
-    first_row = lax.axis_index("row") * per_device
-    my_scale = lax.dynamic_slice_in_dim(row_scale, first_row, per_device, 0)[:, None]
     weights_all = jnp.concatenate([w_query, key_weight, value_weight], axis=1)
-    projected = lax.psum_scatter(
-        jnp.dot(normed, weights_all, preferred_element_type=jnp.float32),
-        "row",
-        scatter_dimension=0,
-        tiled=True,
-    )
+    partial_all = jnp.dot(normed, weights_all, preferred_element_type=jnp.float32)
+    lanes = jnp.broadcast_to(squares, (squares.shape[0], head_size))
+    projected = scatter_sum(jnp.concatenate([partial_all, lanes], axis=1), "row", row_size)
+    my_scale = lax.rsqrt(projected[:, query_width + 2 * kv_width :][:, :1] / MODEL_WIDTH + 1e-05)
     query_part = projected[:, :query_width]
     key_part = projected[:, query_width : query_width + kv_width]
-    value_part = projected[:, query_width + kv_width :]
+    value_part = projected[:, query_width + kv_width : query_width + 2 * kv_width]
     query_rotated_rows = apply_rotation(
         (query_part * my_scale).reshape(per_device, kv_heads * group_size, head_size), lengths
     )
@@ -103,13 +150,11 @@
         per_device, kv_heads * group_size * head_size
     )
     partial_out = jnp.dot(
-        lax.all_gather(heads_out, "row", axis=0, tiled=True),
+        gather_rows(heads_out, "row", row_size),
         w_output,
         preferred_element_type=jnp.float32,
     )
-    return lax.psum_scatter(partial_out, "col", scatter_dimension=0, tiled=True).astype(
-        jnp.bfloat16
-    )
+    return scatter_sum(partial_out, "col", col_size).astype(jnp.bfloat16)
 
 
 def solution(mesh):
@@ -124,6 +169,7 @@
         P(("rep", "row"), None, "col"),
         P(("rep", "row")),
     )
+    sized = functools.partial(body, mesh.shape["row"], mesh.shape["col"])
     return jax.shard_map(
-        body, mesh=mesh, in_specs=placed, out_specs=P(("rep", "col"), "row"), check_vma=False
+        sized, mesh=mesh, in_specs=placed, out_specs=P(("rep", "col"), "row"), check_vma=False
     )

time: 71.2 us -> 43.2 us (0.61)
  blocking collectives: 45 us -> 0 us
  starting transfers between devices: 0 us -> 12.4 us
  waiting for transfers between devices: 0 us -> 9.57 us
  local copies, waits for them, and re-layouts: 4.3 us -> 0.65 us
  other arithmetic: 3.99 us -> 2.18 us
    unnamed x2 -> x0, blocking collectives: 31.9 us -> none
    all_gather x1 -> x0, blocking collectives: 13.1 us -> none  [body(): lax.all_gather(heads_out, 'row', axis=0, tiled=True)]
    ppermute x0 -> x9, starting transfers between devices: none -> 12.4 us  [swap_with(): return lax.ppermute(values, axis, [(i, i ^ mask) for i in range(size)])]
    ppermute x0 -> x9, waiting for transfers between devices: none -> 9.57 us  [swap_with(): return lax.ppermute(values, axis, [(i, i ^ mask) for i in range(size)])]
    unnamed x7 -> x5, local copies, waits for them, and re-layouts: 2.52 us -> 0.02 us
    convert_element_type x1, other arithmetic: 1.36 us -> 0.01 us  [body(): tail_new = value_request_rows.astype(jnp.float32)[:, :, None, :]]
    mul x1, other arithmetic: 1.29 us -> 0.01 us  [body(): query_part * my_scale]
    convert_element_type x1 -> x0, local copies, waits for them, and re-layouts: 1.19 us -> none  [body(): lax.psum_scatter(partial_out, 'col', scatter_dimension=0, tiled=True)]
  transfers between devices with their start and end apart: 0 -> 9, of which waited for: 0 -> 6; matrix products, arithmetic and copies ran while one was open for 0% -> 0% of each run, Pallas kernels for 0% -> 0%
where the time goes in v1:
time: 43.2 us; the launch traced here: 43 us
  matrix products  16.8 us (39%)
  starting transfers between devices  12.4 us (29%)
  waiting for transfers between devices  9.57 us (22%)
  other arithmetic  2.18 us (5%)
  between operations  1.47 us (3%)
  local copies, waits for them, and re-layouts  0.65 us (2%)
    ppermute x9, starting transfers between devices, swap_with(): return lax.ppermute(values, axis, [(i, i ^ mask) for i in range(size)])  12.4 us
    ppermute x9, waiting for transfers between devices, swap_with(): return lax.ppermute(values, axis, [(i, i ^ mask) for i in range(size)])  9.57 us
    dot_general x1, matrix products, body(): jnp.dot(gather_rows(heads_out, 'row', row_size), w_output, preferred_elem...  8.05 us
    dot_general x1, matrix products, body(): jnp.dot(normed, weights_all, preferred_element_type=jnp.float32)  7.86 us
    reduce_sum x1, other arithmetic, body(): squares = jnp.sum(inputs * inputs, axis=1, keepdims=True)  0.96 us
  transfers between devices with their start and end apart: 9, of which 6 were waited for; matrix products, arithmetic and copies ran while one was open for 0% of the time, Pallas kernels for 0%

profile of v1, /device:TPU:0, one launch (start us, length us, event | category | flops | bytes accessed | tf_op | source)
XLA Modules:
  0.0 43.0 jit_solution(7370435538511255200)
XLA Ops:
  0.0 1.0 %fusion.13 = f32[4]{0:T(128)S(1)} fusion(bf16[4,4096]{1,0:T(4,128)(2,1)} %param.9), kind=kLoop, calls=%fused_computation.25 | loop fusion | flops 49148 | bytes 32784 | tf_op jit(solution)/shard_map/reduce_sum | solution.py:97
  1.0 7.9 %fusion = f32[4,2304]{1,0:T(4,128)S(1)} fusion(bf16[4096,128]{1,0:T(8,128)(2,1)} %param.13, bf16[4096,128]{1,0:T(8,128)(2,1)} %param.12, bf16[4096,2048]{1,0:T(8,128)(2,1)} %param.11, bf16[4,4096]{1,0:T(4,128)(2,1)} %param.9, f32[4096]{0:T(1024)} %param.10), kind=kOutput, calls=%fused_computation | convolution fusion | flops 132169728 | bytes 18960384 | tf_op jit(solution)/shard_map/dot_general | solution.py:100
  9.0 5.1 %collective-permute-start = (f32[1,2432]{1,0:T(1,128)S(1)}, f32[1,2432]{1,0:T(1,128)S(1)}, u32[]{:S(2)}, u32[]{:S(2)}) collective-permute-start(f32[1,2432]{1,0:T(1,128)S(1)} %get-tuple-element.8), channel_id=1, source_target_pairs={{0,12},{4,8},{8,4},{12,0},{1,13},{5,9},{9,5},{13,1},{2,14},{6,10},... | collective-permute-start | bytes 29192 | tf_op jit(solution)/shard_map/ppermute | solution.py:40
  14.1 0.6 %collective-permute-start.2 = (f32[1,2432]{1,0:T(1,128)S(1)}, f32[1,2432]{1,0:T(1,128)S(1)}, u32[]{:S(2)}, u32[]{:S(2)}) collective-permute-start(f32[1,2432]{1,0:T(1,128)S(1)} %get-tuple-element.10), channel_id=1, source_target_pairs={{0,4},{4,0},{8,12},{12,8},{1,5},{5,1},{9,13},{13,9},{2,6},{6,2},{1... | collective-permute-start | bytes 29192 | tf_op jit(solution)/shard_map/ppermute | solution.py:40
  15.4 0.3 collective-permute-done
  15.7 2.9 %collective-permute-done.1 = f32[1,2432]{1,0:T(1,128)S(1)} collective-permute-done((f32[1,2432]{1,0:T(1,128)S(1)}, f32[1,2432]{1,0:T(1,128)S(1)}, u32[]{:S(2)}, u32[]{:S(2)}) %collective-permute-start.1) | collective-permute-done | bytes 9760 | tf_op jit(solution)/shard_map/ppermute | solution.py:40
  18.7 0.5 %slice.35 = f32[1,1]{1,0:T(1,128)} slice(f32[1,2432]{1,0:T(1,128)S(1)} %add_add_fusion), slice={[0:1], [2304:2305]} | slice | bytes 8 | tf_op jit(solution)/shard_map/slice | solution.py:103
  20.0 0.1 fusion.33
  20.1 0.4 select_reduce_fusion
  20.5 0.2 fusion.51
  20.7 0.2 fusion.11
  20.9 0.3 fusion.7
  21.2 0.1 collective-permute-start.5
  21.3 2.1 %collective-permute-start.4 = (bf16[1,2048]{1,0:T(2,128)(2,1)S(1)}, bf16[1,2048]{1,0:T(2,128)(2,1)S(1)}, u32[]{:S(2)}, u32[]{:S(2)}) collective-permute-start(bf16[1,2048]{1,0:T(2,128)(2,1)S(1)} %bitcast.54), channel_id=1, source_target_pairs={{0,8},{4,12},{8,0},{12,4},{1,9},{5,13},{9,1},{13,5},{2,10},{6,14},... | collective-permute-start | bytes 12296 | tf_op jit(solution)/shard_map/ppermute | solution.py:40
  23.4 2.3 %collective-permute-start.3 = (bf16[1,2048]{1,0:T(2,128)(2,1)S(1)}, bf16[1,2048]{1,0:T(2,128)(2,1)S(1)}, u32[]{:S(2)}, u32[]{:S(2)}) collective-permute-start(bf16[1,2048]{1,0:T(2,128)(2,1)S(1)} %bitcast.55), channel_id=1, source_target_pairs={{0,12},{4,8},{8,4},{12,0},{1,13},{5,9},{9,5},{13,1},{2,14},{6,10},... | collective-permute-start | bytes 12296 | tf_op jit(solution)/shard_map/ppermute | solution.py:40
  25.6 0.2 collective-permute-done.4
  25.9 2.9 %collective-permute-done.3 = bf16[1,2048]{1,0:T(2,128)(2,1)S(1)} collective-permute-done((bf16[1,2048]{1,0:T(2,128)(2,1)S(1)}, bf16[1,2048]{1,0:T(2,128)(2,1)S(1)}, u32[]{:S(2)}, u32[]{:S(2)}) %collective-permute-start.3) | collective-permute-done | bytes 4128 | tf_op jit(solution)/shard_map/ppermute | solution.py:40
  28.9 8.0 %fusion.20 = f32[4,4096]{1,0:T(4,128)S(1)} fusion(bf16[2048,4096]{1,0:T(8,128)(2,1)} %param.14, bf16[1,2048]{1,0:T(2,128)(2,1)S(1)} %get-tuple-element.12, bf16[1,2048]{1,0:T(2,128)(2,1)S(1)} %get-tuple-element.13, bf16[1,2048]{1,0:T(2,128)(2,1)S(1)} %get-tuple-element.14, bf16[1,2048]{1,0:T(2,128)(2,1)S(1)} %get-tuple-element.11), kind=kOutput, calls=%fused_computation.35 | convolution fusion | flops 67174400 | bytes 16859136 | tf_op jit(solution)/shard_map/dot_general | solution.py:152
  37.0 0.1 collective-permute-start.6
  37.0 1.6 %collective-permute-start.8 = (f32[1,4096]{1,0:T(1,128)S(1)}, f32[1,4096]{1,0:T(1,128)S(1)}, u32[]{:S(2)}, u32[]{:S(2)}) collective-permute-start(f32[1,4096]{1,0:T(1,128)S(1)} %get-tuple-element.6), channel_id=1, source_target_pairs={{0,1},{1,0},{2,3},{3,2},{4,5},{5,4},{6,7},{7,6},{8,9},{9,8},{10,11... | collective-permute-start | bytes 49160 | tf_op jit(solution)/shard_map/ppermute | solution.py:40
  38.6 0.5 %collective-permute-start.7 = (f32[1,4096]{1,0:T(1,128)S(1)}, f32[1,4096]{1,0:T(1,128)S(1)}, u32[]{:S(2)}, u32[]{:S(2)}) collective-permute-start(f32[1,4096]{1,0:T(1,128)S(1)} %get-tuple-element.7), channel_id=1, source_target_pairs={{0,2},{1,3},{2,0},{3,1},{4,6},{5,7},{6,4},{7,5},{8,10},{9,11},{10,... | collective-permute-start | bytes 49160 | tf_op jit(solution)/shard_map/ppermute | solution.py:40
  39.2 1.1 %collective-permute-done.6 = f32[1,4096]{1,0:T(1,128)S(1)} collective-permute-done((f32[1,4096]{1,0:T(1,128)S(1)}, f32[1,4096]{1,0:T(1,128)S(1)}, u32[]{:S(2)}, u32[]{:S(2)}) %collective-permute-start.6) | collective-permute-done | bytes 16416 | tf_op jit(solution)/shard_map/ppermute | solution.py:40
  40.3 2.1 %collective-permute-done.7 = f32[1,4096]{1,0:T(1,128)S(1)} collective-permute-done((f32[1,4096]{1,0:T(1,128)S(1)}, f32[1,4096]{1,0:T(1,128)S(1)}, u32[]{:S(2)}, u32[]{:S(2)}) %collective-permute-start.7) | collective-permute-done | bytes 16416 | tf_op jit(solution)/shard_map/ppermute | solution.py:40
  42.4 0.6 %add_convert_fusion = bf16[1,4096]{1,0:T(2,128)(2,1)} fusion(f32[1,4096]{1,0:T(1,128)S(1)} %collective-permute-done.8, f32[1,4096]{1,0:T(1,128)S(1)} %collective-permute-done.7, f32[1,4096]{1,0:T(1,128)S(1)} %collective-permute-done.6, f32[4,4096]{1,0:T(4,128)S(1)} %fusion.20, s32[]{:T(128)S(6)} %select_n.137), kind=kLoop, calls=%fused_computation.43 | loop fusion | flops 16384 | bytes 73732 | tf_op jit(solution)/shard_map/convert_element_type | solution.py:157
  (20 shorter events, 0.4 us)
Async XLA Ops:
  0.0 20.1 %copy-start = (bf16[1,2048,128]{2,1,0:T(8,128)(2,1)S(1)}, bf16[1,2048,128]{2,1,0:T(8,128)(2,1)}, u32[]{:S(2)}) copy-start(bf16[1,2048,128]{2,1,0:T(8,128)(2,1)} %param.15) | copy-start | bytes 1572868
  1.0 19.9 %copy-start.1 = (bf16[1,2048,128]{2,1,0:T(8,128)(2,1)S(1)}, bf16[1,2048,128]{2,1,0:T(8,128)(2,1)}, u32[]{:S(2)}) copy-start(bf16[1,2048,128]{2,1,0:T(8,128)(2,1)} %param.16) | copy-start | bytes 1572868
  9.0 6.8 %collective-permute-start = (f32[1,2432]{1,0:T(1,128)S(1)}, f32[1,2432]{1,0:T(1,128)S(1)}, u32[]{:S(2)}, u32[]{:S(2)}) collective-permute-start(f32[1,2432]{1,0:T(1,128)S(1)} %get-tuple-element.8), channel_id=1, source_target_pairs={{0,12},{4,8},{8,4},{12,0},{1,13},{5,9},{9,5},{13,1},{2,14},{6,10},... | collective-permute-start | bytes 29192 | tf_op jit(solution)/shard_map/ppermute | solution.py:40
  14.1 4.6 %collective-permute-start.1 = (f32[1,2432]{1,0:T(1,128)S(1)}, f32[1,2432]{1,0:T(1,128)S(1)}, u32[]{:S(2)}, u32[]{:S(2)}) collective-permute-start(f32[1,2432]{1,0:T(1,128)S(1)} %get-tuple-element.9), channel_id=1, source_target_pairs={{0,8},{4,12},{8,0},{12,4},{1,9},{5,13},{9,1},{13,5},{2,10},{6,14},... | collective-permute-start | bytes 29192 | tf_op jit(solution)/shard_map/ppermute | solution.py:40
  14.1 4.6 %collective-permute-start.2 = (f32[1,2432]{1,0:T(1,128)S(1)}, f32[1,2432]{1,0:T(1,128)S(1)}, u32[]{:S(2)}, u32[]{:S(2)}) collective-permute-start(f32[1,2432]{1,0:T(1,128)S(1)} %get-tuple-element.10), channel_id=1, source_target_pairs={{0,4},{4,0},{8,12},{12,8},{1,5},{5,1},{9,13},{13,9},{2,6},{6,2},{1... | collective-permute-start | bytes 29192 | tf_op jit(solution)/shard_map/ppermute | solution.py:40
  21.2 4.5 %collective-permute-start.5 = (bf16[1,2048]{1,0:T(2,128)(2,1)S(1)}, bf16[1,2048]{1,0:T(2,128)(2,1)S(1)}, u32[]{:S(2)}, u32[]{:S(2)}) collective-permute-start(bf16[1,2048]{1,0:T(2,128)(2,1)S(1)} %bitcast.53), channel_id=1, source_target_pairs={{0,4},{4,0},{8,12},{12,8},{1,5},{5,1},{9,13},{13,9},{2,6},{6,2},{1... | collective-permute-start | bytes 12296 | tf_op jit(solution)/shard_map/ppermute | solution.py:40
  21.3 4.6 %collective-permute-start.4 = (bf16[1,2048]{1,0:T(2,128)(2,1)S(1)}, bf16[1,2048]{1,0:T(2,128)(2,1)S(1)}, u32[]{:S(2)}, u32[]{:S(2)}) collective-permute-start(bf16[1,2048]{1,0:T(2,128)(2,1)S(1)} %bitcast.54), channel_id=1, source_target_pairs={{0,8},{4,12},{8,0},{12,4},{1,9},{5,13},{9,1},{13,5},{2,10},{6,14},... | collective-permute-start | bytes 12296 | tf_op jit(solution)/shard_map/ppermute | solution.py:40
  23.4 5.4 %collective-permute-start.3 = (bf16[1,2048]{1,0:T(2,128)(2,1)S(1)}, bf16[1,2048]{1,0:T(2,128)(2,1)S(1)}, u32[]{:S(2)}, u32[]{:S(2)}) collective-permute-start(bf16[1,2048]{1,0:T(2,128)(2,1)S(1)} %bitcast.55), channel_id=1, source_target_pairs={{0,12},{4,8},{8,4},{12,0},{1,13},{5,9},{9,5},{13,1},{2,14},{6,10},... | collective-permute-start | bytes 12296 | tf_op jit(solution)/shard_map/ppermute | solution.py:40
  37.0 3.4 %collective-permute-start.6 = (f32[1,4096]{1,0:T(1,128)S(1)}, f32[1,4096]{1,0:T(1,128)S(1)}, u32[]{:S(2)}, u32[]{:S(2)}) collective-permute-start(f32[1,4096]{1,0:T(1,128)S(1)} %get-tuple-element.5), channel_id=1, source_target_pairs={{0,3},{1,2},{2,1},{3,0},{4,7},{5,6},{6,5},{7,4},{8,11},{9,10},{10,... | collective-permute-start | bytes 49160 | tf_op jit(solution)/shard_map/ppermute | solution.py:40
  37.0 3.3 %collective-permute-start.8 = (f32[1,4096]{1,0:T(1,128)S(1)}, f32[1,4096]{1,0:T(1,128)S(1)}, u32[]{:S(2)}, u32[]{:S(2)}) collective-permute-start(f32[1,4096]{1,0:T(1,128)S(1)} %get-tuple-element.6), channel_id=1, source_target_pairs={{0,1},{1,0},{2,3},{3,2},{4,5},{5,4},{6,7},{7,6},{8,9},{9,8},{10,11... | collective-permute-start | bytes 49160 | tf_op jit(solution)/shard_map/ppermute | solution.py:40
  38.6 3.7 %collective-permute-start.7 = (f32[1,4096]{1,0:T(1,128)S(1)}, f32[1,4096]{1,0:T(1,128)S(1)}, u32[]{:S(2)}, u32[]{:S(2)}) collective-permute-start(f32[1,4096]{1,0:T(1,128)S(1)} %get-tuple-element.7), channel_id=1, source_target_pairs={{0,2},{1,3},{2,0},{3,1},{4,6},{5,7},{6,4},{7,5},{8,10},{9,11},{10,... | collective-permute-start | bytes 49160 | tf_op jit(solution)/shard_map/ppermute | solution.py:40

commit v2 on v1

--- a/solution.py
+++ b/solution.py
@@ -3,12 +3,15 @@
 import jax
 import jax.numpy as jnp
 from jax import lax
+from jax.experimental import pallas as pl
+from jax.experimental.pallas import tpu as pltpu
 from jax.sharding import PartitionSpec as P
 
 MODEL_WIDTH = 16384
 QUERY_HEADS = 64
 KEY_VALUE_HEADS = 4
 HEAD_WIDTH = 128
+REQUEST_COUNT = 4
 
 
 def apply_rotation(values, positions):
@@ -26,6 +29,11 @@
 
 
 DIRECT_LIMIT = 8
+MIB = 1024 * 1024
+VMEM_HELD = 26 * MIB
+PRIORITY = 1
+BLOCK = 512
+AHEAD = 4
 
 
 def is_direct(size):
@@ -71,6 +79,222 @@
             block = jnp.where((me ^ mask) == place, blocks[mask], block)
         ordered.append(block)
     return jnp.concatenate(ordered, axis=0)
+
+
+def in_hbm(array):
+    return pltpu.with_memory_space_constraint(array, pltpu.HBM)
+
+
+def project_kernel(row_size, block, ahead, hidden, gain, w_query, w_key, w_value, *refs):
+    shares = refs[:row_size]
+    inputs_near, gain_near, query_buffer, key_buffer, value_buffer, sems, small, left, total = refs[
+        row_size:
+    ]
+    requests, depth = hidden.shape
+    query_width, kv_width = w_query.shape[1], w_key.shape[1]
+    steps = depth // block
+    wide = depth // min(4, steps)
+    first = [
+        pltpu.make_async_copy(hidden, inputs_near, small.at[0]),
+        pltpu.make_async_copy(gain, gain_near, small.at[1]),
+    ]
+    stages = []
+    for step in range(steps):
+        start = step * block
+        group = []
+        if start % wide == 0:
+            rows = pl.ds(start, wide)
+            for lane, (far, near) in enumerate(((w_key, key_buffer), (w_value, value_buffer))):
+                copy = pltpu.make_async_copy(
+                    far.at[rows], near.at[rows], sems.at[1 + lane, start // wide]
+                )
+                group.append((copy, 1 + lane, near, start, wide))
+        rows = pl.ds(start, block)
+        copy = pltpu.make_async_copy(w_query.at[rows], query_buffer.at[rows], sems.at[0, step])
+        group.append((copy, 0, query_buffer, start, block))
+        stages.append(group)
+    for copy in first:
+        copy.start()
+    for group in stages[:ahead]:
+        for item in group:
+            item[0].start(priority=PRIORITY)
+    for copy in first:
+        copy.wait()
+    inputs = inputs_near[...].astype(jnp.float32)
+    left[...] = jnp.zeros_like(left)
+    left[:requests, :] = inputs * gain_near[...]
+    normed = left[...].astype(jnp.bfloat16)
+    squares = jnp.sum(inputs * inputs, axis=1, keepdims=True)
+    sums = [None, None, None]
+    for step, group in enumerate(stages):
+        for copy, which, near, start, size in group:
+            copy.wait()
+            if which == 0 and step + ahead < steps:
+                for item in stages[step + ahead]:
+                    item[0].start(priority=PRIORITY)
+            part = jnp.dot(
+                normed[:, start : start + size],
+                near[start : start + size, :],
+                preferred_element_type=jnp.float32,
+            )
+            sums[which] = part if sums[which] is None else sums[which] + part
+    total[:, :query_width] = sums[0]
+    total[:, query_width : query_width + kv_width] = sums[1]
+    total[:, query_width + kv_width : query_width + 2 * kv_width] = sums[2]
+    total[:requests, query_width + 2 * kv_width :] = jnp.broadcast_to(
+        squares, (requests, HEAD_WIDTH)
+    )
+    here = lax.axis_index("row")
+    for mask in range(row_size):
+        shares[mask][...] = total[pl.ds(here ^ mask, 1), :]
+
+
+def project_in(hidden_in, norm_gain, w_query, key_weight, value_weight):
+    row_size = hidden_in.shape[0]
+    depth, query_width = w_query.shape
+    kv_width = key_weight.shape[1]
+    block = min(depth, BLOCK)
+    steps = depth // block
+    width = query_width + 2 * kv_width + HEAD_WIDTH
+    near = pl.BlockSpec(memory_space=pltpu.VMEM)
+    far = pl.BlockSpec(memory_space=pltpu.HBM)
+    size = 2 * depth * (query_width + 2 * kv_width)
+    return pl.pallas_call(
+        functools.partial(project_kernel, row_size, block, AHEAD),
+        out_shape=[jax.ShapeDtypeStruct((1, width), jnp.float32)] * row_size,
+        in_specs=[far] * 5,
+        out_specs=[near] * row_size,
+        scratch_shapes=[
+            pltpu.VMEM((row_size, depth), jnp.bfloat16),
+            pltpu.VMEM((1, depth), jnp.float32),
+            pltpu.VMEM((depth, query_width), jnp.bfloat16),
+            pltpu.VMEM((depth, kv_width), jnp.bfloat16),
+            pltpu.VMEM((depth, kv_width), jnp.bfloat16),
+            pltpu.SemaphoreType.DMA((3, steps)),
+            pltpu.SemaphoreType.DMA((2,)),
+            pltpu.VMEM((8, depth), jnp.float32),
+            pltpu.VMEM((8, width), jnp.float32),
+        ],
+        compiler_params=pltpu.CompilerParams(vmem_limit_bytes=VMEM_HELD),
+        cost_estimate=pl.CostEstimate(
+            flops=row_size * size, bytes_accessed=size, transcendentals=0
+        ),
+        name="project_in",
+    )(*map(in_hbm, (hidden_in, norm_gain.reshape(1, depth), w_query, key_weight, value_weight)))
+
+
+def attend_kernel(row_size, *refs):
+    shares = refs[:row_size]
+    length, cosine, sine, keys, values, heads, rows = refs[row_size:]
+    heads_count, width = heads.shape
+    summed = shares[0][...]
+    for part in shares[1:]:
+        summed = summed + part[...]
+    query_width = heads_count * width
+    squares = summed[:, query_width + 2 * width :]
+    scale = lax.rsqrt(squares / MODEL_WIDTH + 1e-05)
+    for head in range(heads_count):
+        rows[head : head + 1, :] = summed[:, head * width : (head + 1) * width] * scale
+    key_row = summed[:, query_width : query_width + width] * scale
+    value_row = summed[:, query_width + width : query_width + 2 * width] * scale
+    rows[heads_count : heads_count + 8, :] = jnp.broadcast_to(key_row, (8, width))
+    both = rows[...]
+    turned = both * cosine[...] + pltpu.roll(both, width // 2, 1) * sine[...]
+    turned = turned.astype(jnp.bfloat16)
+    query = turned[:heads_count]
+    key_new = turned[heads_count : heads_count + 8].astype(jnp.float32)[:1]
+    value_new = value_row.astype(jnp.bfloat16).astype(jnp.float32)
+    inverse = 1.0 / width**0.5
+    scores = (
+        lax.dot_general(
+            query, keys[...], (((1,), (1,)), ((), ())), preferred_element_type=jnp.float32
+        )
+        * inverse
+    )
+    score_new = (
+        jnp.sum(query.astype(jnp.float32) * key_new, axis=1, keepdims=True) * inverse
+    )
+    place = lax.broadcasted_iota(jnp.int32, scores.shape, 1)
+    live = place < length[0]
+    scores = jnp.where(live, scores, -jnp.inf)
+    largest = jnp.maximum(jnp.max(scores, axis=1, keepdims=True), score_new)
+    expo = jnp.exp(scores - largest)
+    expo_new = jnp.exp(score_new - largest)
+    part = 1.0 / (jnp.sum(expo, axis=1, keepdims=True) + expo_new)
+    probs = (expo * part).astype(jnp.bfloat16)
+    prob_new = (expo_new * part).astype(jnp.bfloat16).astype(jnp.float32)
+    mixed = jnp.dot(probs, values[...], preferred_element_type=jnp.float32)
+    heads[...] = (mixed + prob_new * value_new).astype(jnp.bfloat16)
+
+
+def attend(shares, lengths, keys, values, heads_count):
+    row_size = len(shares)
+    slots, width = keys.shape
+    half = width // 2
+    frequency = 500000.0 ** (-(jnp.arange(half, dtype=jnp.float32) * 2.0 / width))
+    angles = lengths.astype(jnp.float32)[:, None] * frequency[None, :]
+    cosine, sine = jnp.cos(angles), jnp.sin(angles)
+    cosine = jnp.concatenate([cosine, cosine], axis=1)
+    sine = jnp.concatenate([-sine, sine], axis=1)
+    near = pl.BlockSpec(memory_space=pltpu.VMEM)
+    return pl.pallas_call(
+        functools.partial(attend_kernel, row_size),
+        out_shape=jax.ShapeDtypeStruct((heads_count, width), jnp.bfloat16),
+        in_specs=[near] * row_size + [pl.BlockSpec(memory_space=pltpu.SMEM)] + [near] * 4,
+        out_specs=near,
+        scratch_shapes=[pltpu.VMEM((heads_count + 8, width), jnp.float32)],
+        compiler_params=pltpu.CompilerParams(vmem_limit_bytes=4 * MIB),
+        cost_estimate=pl.CostEstimate(
+            flops=4 * heads_count * slots * width,
+            bytes_accessed=4 * slots * width,
+            transcendentals=heads_count * slots,
+        ),
+        name="attend",
+    )(*shares, lengths, cosine, sine, keys, values)
+
+
+def output_kernel(row_size, col_size, chunk, *refs):
+    heads = refs[:row_size]
+    weight = refs[row_size]
+    shares = refs[row_size + 1 : row_size + 1 + col_size]
+    left, total = refs[row_size + 1 + col_size :]
+    count = heads[0].shape[0]
+    width = heads[0].shape[1]
+    left[...] = jnp.zeros_like(left)
+    for slot in range(row_size):
+        rows = heads[slot][...].astype(jnp.float32)
+        for head in range(count):
+            left[slot : slot + 1, head * width : (head + 1) * width] = rows[head : head + 1, :]
+    lhs = left[...].astype(jnp.bfloat16)
+    for start in range(0, weight.shape[1], chunk):
+        total[:, start : start + chunk] = jnp.dot(
+            lhs, weight[:, start : start + chunk], preferred_element_type=jnp.float32
+        )
+    here = lax.axis_index("row")
+    lane = lax.axis_index("col")
+    for mask in range(col_size):
+        shares[mask][...] = total[pl.ds((lane ^ mask) ^ here, 1), :]
+
+
+def project_out(blocks, w_output, col_size):
+    row_size = len(blocks)
+    depth, width = w_output.shape
+    whole = pl.BlockSpec(memory_space=pltpu.VMEM)
+    return pl.pallas_call(
+        functools.partial(output_kernel, row_size, col_size, min(width, 512)),
+        out_shape=[jax.ShapeDtypeStruct((1, width), jnp.float32)] * col_size,
+        in_specs=[whole] * (row_size + 1),
+        out_specs=[whole] * col_size,
+        scratch_shapes=[
+            pltpu.VMEM((8, depth), jnp.float32),
+            pltpu.VMEM((8, width), jnp.float32),
+        ],
+        compiler_params=pltpu.CompilerParams(vmem_limit_bytes=4 * MIB),
+        cost_estimate=pl.CostEstimate(
+            flops=2 * row_size * depth * width, bytes_accessed=2 * depth * width, transcendentals=0
+        ),
+        name="project_out",
+    )(*blocks, w_output)
 
 
 def body(
@@ -157,6 +381,42 @@
     return scatter_sum(partial_out, "col", col_size).astype(jnp.bfloat16)
 
 
+def direct_body(
+    size,
+    hidden_in,
+    norm_gain,
+    w_query,
+    key_weight,
+    value_weight,
+    w_output,
+    stored_keys,
+    stored_values,
+    lengths,
+):
+    head_size = HEAD_WIDTH
+    parts = project_in(hidden_in, norm_gain, w_query, key_weight, value_weight)
+    shares = [parts[0]] + [
+        swap_with(parts[mask], "row", size, mask) for mask in partner_order(size)
+    ]
+    mine = attend(
+        shares, lengths, stored_keys[0], stored_values[0], w_query.shape[1] // head_size
+    )
+    blocks = [mine] + [None] * (size - 1)
+    for mask in partner_order(size):
+        blocks[mask] = swap_with(mine, "row", size, mask)
+    parts = project_out(blocks, w_output, size)
+    received = [swap_with(parts[mask], "col", size, mask) for mask in partner_order(size)]
+    total = parts[0]
+    for part in received:
+        total = total + part
+    return total.astype(jnp.bfloat16)
+
+
+def fits_direct(mesh):
+    size = mesh.shape["row"]
+    return is_direct(size) and size == mesh.shape["col"] == KEY_VALUE_HEADS == REQUEST_COUNT
+
+
 def solution(mesh):
     placed = (
         P("rep", "row"),
@@ -169,7 +429,10 @@
         P(("rep", "row"), None, "col"),
         P(("rep", "row")),
     )
-    sized = functools.partial(body, mesh.shape["row"], mesh.shape["col"])
+    if fits_direct(mesh):
+        sized = functools.partial(direct_body, mesh.shape["row"])
+    else:
+        sized = functools.partial(body, mesh.shape["row"], mesh.shape["col"])
     return jax.shard_map(
         sized, mesh=mesh, in_specs=placed, out_specs=P(("rep", "col"), "row"), check_vma=False
     )

time: 43.2 us -> 30.9 us (0.72)
  matrix products: 16.8 us -> 0 us
  Pallas kernels: 0 us -> 10.4 us
  waiting for transfers between devices: 9.57 us -> 6.58 us
  other arithmetic: 2.18 us -> 0.89 us
  between operations: 1.47 us -> 0.7 us
  local copies, waits for them, and re-layouts: 0.65 us -> 0.01 us
    dot_general x5 -> x0, matrix products: 16.8 us -> none  [the longest x1 8.05 us: body(): jnp.dot(gather_rows(heads_out, 'row', row_size), w_output, preferred_elem...]
    pallas_call x0 -> x3, Pallas kernels: none -> 10.4 us  [the longest x1 7.44 us: project_in(): pl.pallas_call(functools.partial(project_kernel, row_size, block, AHEAD),...]
    ppermute x9, waiting for transfers between devices: 9.57 us -> 6.58 us  [swap_with(): return lax.ppermute(values, axis, [(i, i ^ mask) for i in range(size)])]
    reduce_sum x2 -> x0, other arithmetic: 1.19 us -> none  [the longest x1 0.96 us: body(): squares = jnp.sum(inputs * inputs, axis=1, keepdims=True)]
    slice x1 -> x0, local copies, waits for them, and re-layouts: 0.51 us -> none  [body(): projected[:, query_width + 2 * kv_width:][:, :1] / MODEL_WIDTH + 1e-05]
  transfers between devices with their start and end apart: 9 -> 9, of which waited for: 6 -> 6; matrix products, arithmetic and copies ran while one was open for 0% -> 1% of each run, Pallas kernels for 0% -> 0%
where the time goes in v2:
time: 30.9 us; the launch traced here: 30.7 us
  starting transfers between devices  12.1 us (39%)
  Pallas kernels  10.4 us (34%)
  waiting for transfers between devices  6.58 us (21%)
  other arithmetic  0.89 us (3%)
  between operations  0.7 us (2%)
    ppermute x9, starting transfers between devices, swap_with(): return lax.ppermute(values, axis, [(i, i ^ mask) for i in range(size)])  12.1 us
    pallas_call x1, Pallas kernels, project_in(): pl.pallas_call(functools.partial(project_kernel, row_size, block, AHEAD),...  7.44 us
    ppermute x9, waiting for transfers between devices, swap_with(): return lax.ppermute(values, axis, [(i, i ^ mask) for i in range(size)])  6.58 us
    pallas_call x1, Pallas kernels, project_out(): pl.pallas_call(functools.partial(output_kernel, row_size, col_size, min(w...  2.3 us
    pallas_call x1, Pallas kernels, attend(): pl.pallas_call(functools.partial(attend_kernel, row_size), out_shape=jax....  0.67 us
    convert_element_type x1, other arithmetic, direct_body(): return total.astype(jnp.bfloat16)  0.64 us
  transfers between devices with their start and end apart: 9, of which 6 were waited for; matrix products, arithmetic and copies ran while one was open for 1% of the time, Pallas kernels for 0%

profile of v2, /device:TPU:0, one launch (start us, length us, event | category | flops | bytes accessed | tf_op | source)
XLA Modules:
  0.0 30.7 jit_solution(14297566433219624474)
XLA Ops:
  0.0 7.4 %project_in.1 = (f32[1,2432]{1,0:T(1,128)S(1)}, f32[1,2432]{1,0:T(1,128)S(1)}, f32[1,2432]{1,0:T(1,128)S(1)}, f32[1,2432]{1,0:T(1,128)S(1)}) custom-call(bf16[4,4096]{1,0:T(4,128)(2,1)} %hidden.1, f32[1,4096]{1,0:T(1,128)} %bitcast.6, bf16[4096,2048]{1,0:T(8,128)(2,1)} %w_query.1, bf16[4096,128]{1,0:T(8,128)(2,1)} %w_key.1, bf16[4096,128]{1,0:T(8,128)(2,1)} %w_value.1), custom_call_target="tpu_custom_call" | custom-call | flops 75497472 | bytes 18874368 | tf_op jit(solution)/shard_map/project_in/pallas_call | solution.py:162
  7.5 5.1 %collective-permute-start = (f32[1,2432]{1,0:T(1,128)S(1)}, f32[1,2432]{1,0:T(1,128)S(1)}, u32[]{:S(2)}, u32[]{:S(2)}) collective-permute-start(f32[1,2432]{1,0:T(1,128)S(1)} %get-tuple-element.14), channel_id=1, source_target_pairs={{0,12},{4,8},{8,4},{12,0},{1,13},{5,9},{9,5},{13,1},{2,14},{6,10},... | collective-permute-start | bytes 29192 | tf_op jit(solution)/shard_map/ppermute | solution.py:48
  12.6 0.0 collective-permute-start.1
  12.6 0.6 %collective-permute-start.2 = (f32[1,2432]{1,0:T(1,128)S(1)}, f32[1,2432]{1,0:T(1,128)S(1)}, u32[]{:S(2)}, u32[]{:S(2)}) collective-permute-start(f32[1,2432]{1,0:T(1,128)S(1)} %get-tuple-element.16), channel_id=1, source_target_pairs={{0,4},{4,0},{8,12},{12,8},{1,5},{5,1},{9,13},{13,9},{2,6},{6,2},{1... | collective-permute-start | bytes 29192 | tf_op jit(solution)/shard_map/ppermute | solution.py:48
  13.9 0.1 fusion.2
  13.9 0.1 fusion
  14.0 0.1 pad_maximum_fusion.refs_5_
  14.1 0.1 pad_maximum_fusion.1.refs_6_
  14.1 0.1 collective-permute-done.refs_1_
  14.2 2.9 %collective-permute-done.1.refs_2_ = f32[1,2432]{1,0:T(1,128)S(1)} collective-permute-done((f32[1,2432]{1,0:T(1,128)S(1)}, f32[1,2432]{1,0:T(1,128)S(1)}, u32[]{:S(2)}, u32[]{:S(2)}) %collective-permute-start.1) | collective-permute-done | bytes 9760 | tf_op jit(solution)/shard_map/ppermute | solution.py:48
  17.2 0.7 %attend.1.refs_0_ = bf16[16,128]{1,0:T(8,128)(2,1)S(1)} custom-call(f32[1,2432]{1,0:T(1,128)S(1)} %get-tuple-element.13.refs_0_, f32[1,2432]{1,0:T(1,128)S(1)} %collective-permute-done.refs_1_, f32[1,2432]{1,0:T(1,128)S(1)} %collective-permute-done.1.refs_2_, f32[1,2432]{1,0:T(1,128)S(1)} %collective-permute-done.2.refs_3_, s32[1]{0:T(128)S(6)} %copy.10.refs_4_, ...), custom_call_target="tpu_custom_call" | custom-call | flops 16777216 | bytes 1048576 | tf_op jit(solution)/shard_map/attend/pallas_call | solution.py:240
  17.8 1.5 %collective-permute-start.5 = (bf16[16,128]{1,0:T(8,128)(2,1)S(1)}, bf16[16,128]{1,0:T(8,128)(2,1)S(1)}, u32[]{:S(2)}, u32[]{:S(2)}) collective-permute-start(bf16[16,128]{1,0:T(8,128)(2,1)S(1)} %attend.1.refs_0_), channel_id=1, source_target_pairs={{0,12},{4,8},{8,4},{12,0},{1,13},{5,9},{9,5},{13,1},{2,14},{6,10},... | collective-permute-start | bytes 12296 | tf_op jit(solution)/shard_map/ppermute | solution.py:48
  19.3 0.6 %collective-permute-start.4 = (bf16[16,128]{1,0:T(8,128)(2,1)S(1)}, bf16[16,128]{1,0:T(8,128)(2,1)S(1)}, u32[]{:S(2)}, u32[]{:S(2)}) collective-permute-start(bf16[16,128]{1,0:T(8,128)(2,1)S(1)} %attend.1.refs_0_), channel_id=1, source_target_pairs={{0,8},{4,12},{8,0},{12,4},{1,9},{5,13},{9,1},{13,5},{2,10},{6,14},... | collective-permute-start | bytes 12296 | tf_op jit(solution)/shard_map/ppermute | solution.py:48
  20.0 2.3 %collective-permute-start.3 = (bf16[16,128]{1,0:T(8,128)(2,1)S(1)}, bf16[16,128]{1,0:T(8,128)(2,1)S(1)}, u32[]{:S(2)}, u32[]{:S(2)}) collective-permute-start(bf16[16,128]{1,0:T(8,128)(2,1)S(1)} %attend.1.refs_0_), channel_id=1, source_target_pairs={{0,4},{4,0},{8,12},{12,8},{1,5},{5,1},{9,13},{13,9},{2,6},{6,2},{1... | collective-permute-start | bytes 12296 | tf_op jit(solution)/shard_map/ppermute | solution.py:48
  22.3 1.0 %collective-permute-done.5.refs_3_ = bf16[16,128]{1,0:T(8,128)(2,1)S(1)} collective-permute-done((bf16[16,128]{1,0:T(8,128)(2,1)S(1)}, bf16[16,128]{1,0:T(8,128)(2,1)S(1)}, u32[]{:S(2)}, u32[]{:S(2)}) %collective-permute-start.5) | collective-permute-done | bytes 4128 | tf_op jit(solution)/shard_map/ppermute | solution.py:48
  23.3 0.6 %collective-permute-done.4.refs_2_ = bf16[16,128]{1,0:T(8,128)(2,1)S(1)} collective-permute-done((bf16[16,128]{1,0:T(8,128)(2,1)S(1)}, bf16[16,128]{1,0:T(8,128)(2,1)S(1)}, u32[]{:S(2)}, u32[]{:S(2)}) %collective-permute-start.4) | collective-permute-done | bytes 4128 | tf_op jit(solution)/shard_map/ppermute | solution.py:48
  23.8 0.0 collective-permute-done.3.refs_1_
  23.9 2.3 %project_out.1 = (f32[1,4096]{1,0:T(1,128)S(1)}, f32[1,4096]{1,0:T(1,128)S(1)}, f32[1,4096]{1,0:T(1,128)S(1)}, f32[1,4096]{1,0:T(1,128)S(1)}) custom-call(bf16[16,128]{1,0:T(8,128)(2,1)S(1)} %attend.1.refs_0_, bf16[16,128]{1,0:T(8,128)(2,1)S(1)} %collective-permute-done.3.refs_1_, bf16[16,128]{1,0:T(8,128)(2,1)S(1)} %collective-permute-done.4.refs_2_, ...), custom_call_target="tpu_custom_call" | custom-call | flops 67108864 | bytes 16777216 | tf_op jit(solution)/shard_map/project_out/pallas_call | solution.py:283
  26.2 0.1 collective-permute-start.6
  26.3 1.6 %collective-permute-start.7 = (f32[1,4096]{1,0:T(1,128)S(1)}, f32[1,4096]{1,0:T(1,128)S(1)}, u32[]{:S(2)}, u32[]{:S(2)}) collective-permute-start(f32[1,4096]{1,0:T(1,128)S(1)} %get-tuple-element.19), channel_id=1, source_target_pairs={{0,2},{1,3},{2,0},{3,1},{4,6},{5,7},{6,4},{7,5},{8,10},{9,11},{10,... | collective-permute-start | bytes 49160 | tf_op jit(solution)/shard_map/ppermute | solution.py:48
  27.8 0.3 collective-permute-start.8
  28.1 1.4 %collective-permute-done.6 = f32[1,4096]{1,0:T(1,128)S(1)} collective-permute-done((f32[1,4096]{1,0:T(1,128)S(1)}, f32[1,4096]{1,0:T(1,128)S(1)}, u32[]{:S(2)}, u32[]{:S(2)}) %collective-permute-start.6) | collective-permute-done | bytes 16416 | tf_op jit(solution)/shard_map/ppermute | solution.py:48
  29.6 0.5 %collective-permute-done.7 = f32[1,4096]{1,0:T(1,128)S(1)} collective-permute-done((f32[1,4096]{1,0:T(1,128)S(1)}, f32[1,4096]{1,0:T(1,128)S(1)}, u32[]{:S(2)}, u32[]{:S(2)}) %collective-permute-start.7) | collective-permute-done | bytes 16416 | tf_op jit(solution)/shard_map/ppermute | solution.py:48
  30.1 0.6 %add_convert_fusion = bf16[1,4096]{1,0:T(2,128)(2,1)} fusion(f32[1,4096]{1,0:T(1,128)S(1)} %collective-permute-done.8, f32[1,4096]{1,0:T(1,128)S(1)} %collective-permute-done.7, f32[1,4096]{1,0:T(1,128)S(1)} %get-tuple-element.17, f32[1,4096]{1,0:T(1,128)S(1)} %collective-permute-done.6), kind=kLoop, calls=%fused_computation | loop fusion | flops 16384 | bytes 73728 | tf_op jit(solution)/shard_map/convert_element_type | solution.py:412
  (8 shorter events, 0.0 us)
Async XLA Ops:
  0.0 17.1 %copy-start.2 = (bf16[1,2048,128]{2,1,0:T(8,128)(2,1)S(1)}, bf16[1,2048,128]{2,1,0:T(8,128)(2,1)}, u32[]{:S(2)}) copy-start(bf16[1,2048,128]{2,1,0:T(8,128)(2,1)} %param.16) | copy-start | bytes 1572868
  0.0 17.1 %copy-start.1 = (bf16[1,2048,128]{2,1,0:T(8,128)(2,1)S(1)}, bf16[1,2048,128]{2,1,0:T(8,128)(2,1)}, u32[]{:S(2)}) copy-start(bf16[1,2048,128]{2,1,0:T(8,128)(2,1)} %param.15) | copy-start | bytes 1572868
  0.0 23.9 %copy-start = (bf16[2048,4096]{1,0:T(8,128)(2,1)S(1)}, bf16[2048,4096]{1,0:T(8,128)(2,1)}, u32[]{:S(2)}) copy-start(bf16[2048,4096]{1,0:T(8,128)(2,1)} %refs_4_.2) | copy-start | bytes 50331652
  7.5 6.8 %collective-permute-start = (f32[1,2432]{1,0:T(1,128)S(1)}, f32[1,2432]{1,0:T(1,128)S(1)}, u32[]{:S(2)}, u32[]{:S(2)}) collective-permute-start(f32[1,2432]{1,0:T(1,128)S(1)} %get-tuple-element.14), channel_id=1, source_target_pairs={{0,12},{4,8},{8,4},{12,0},{1,13},{5,9},{9,5},{13,1},{2,14},{6,10},... | collective-permute-start | bytes 29192 | tf_op jit(solution)/shard_map/ppermute | solution.py:48
  12.6 4.6 %collective-permute-start.1 = (f32[1,2432]{1,0:T(1,128)S(1)}, f32[1,2432]{1,0:T(1,128)S(1)}, u32[]{:S(2)}, u32[]{:S(2)}) collective-permute-start(f32[1,2432]{1,0:T(1,128)S(1)} %get-tuple-element.15), channel_id=1, source_target_pairs={{0,8},{4,12},{8,0},{12,4},{1,9},{5,13},{9,1},{13,5},{2,10},{6,14},... | collective-permute-start | bytes 29192 | tf_op jit(solution)/shard_map/ppermute | solution.py:48
  12.6 4.6 %collective-permute-start.2 = (f32[1,2432]{1,0:T(1,128)S(1)}, f32[1,2432]{1,0:T(1,128)S(1)}, u32[]{:S(2)}, u32[]{:S(2)}) collective-permute-start(f32[1,2432]{1,0:T(1,128)S(1)} %get-tuple-element.16), channel_id=1, source_target_pairs={{0,4},{4,0},{8,12},{12,8},{1,5},{5,1},{9,13},{13,9},{2,6},{6,2},{1... | collective-permute-start | bytes 29192 | tf_op jit(solution)/shard_map/ppermute | solution.py:48
  17.8 5.5 %collective-permute-start.5 = (bf16[16,128]{1,0:T(8,128)(2,1)S(1)}, bf16[16,128]{1,0:T(8,128)(2,1)S(1)}, u32[]{:S(2)}, u32[]{:S(2)}) collective-permute-start(bf16[16,128]{1,0:T(8,128)(2,1)S(1)} %attend.1.refs_0_), channel_id=1, source_target_pairs={{0,12},{4,8},{8,4},{12,0},{1,13},{5,9},{9,5},{13,1},{2,14},{6,10},... | collective-permute-start | bytes 12296 | tf_op jit(solution)/shard_map/ppermute | solution.py:48
  19.3 4.5 %collective-permute-start.4 = (bf16[16,128]{1,0:T(8,128)(2,1)S(1)}, bf16[16,128]{1,0:T(8,128)(2,1)S(1)}, u32[]{:S(2)}, u32[]{:S(2)}) collective-permute-start(bf16[16,128]{1,0:T(8,128)(2,1)S(1)} %attend.1.refs_0_), channel_id=1, source_target_pairs={{0,8},{4,12},{8,0},{12,4},{1,9},{5,13},{9,1},{13,5},{2,10},{6,14},... | collective-permute-start | bytes 12296 | tf_op jit(solution)/shard_map/ppermute | solution.py:48
  20.0 3.9 %collective-permute-start.3 = (bf16[16,128]{1,0:T(8,128)(2,1)S(1)}, bf16[16,128]{1,0:T(8,128)(2,1)S(1)}, u32[]{:S(2)}, u32[]{:S(2)}) collective-permute-start(bf16[16,128]{1,0:T(8,128)(2,1)S(1)} %attend.1.refs_0_), channel_id=1, source_target_pairs={{0,4},{4,0},{8,12},{12,8},{1,5},{5,1},{9,13},{13,9},{2,6},{6,2},{1... | collective-permute-start | bytes 12296 | tf_op jit(solution)/shard_map/ppermute | solution.py:48
  26.2 3.4 %collective-permute-start.6 = (f32[1,4096]{1,0:T(1,128)S(1)}, f32[1,4096]{1,0:T(1,128)S(1)}, u32[]{:S(2)}, u32[]{:S(2)}) collective-permute-start(f32[1,4096]{1,0:T(1,128)S(1)} %get-tuple-element.18), channel_id=1, source_target_pairs={{0,3},{1,2},{2,1},{3,0},{4,7},{5,6},{6,5},{7,4},{8,11},{9,10},{10,... | collective-permute-start | bytes 49160 | tf_op jit(solution)/shard_map/ppermute | solution.py:48
  26.3 3.8 %collective-permute-start.7 = (f32[1,4096]{1,0:T(1,128)S(1)}, f32[1,4096]{1,0:T(1,128)S(1)}, u32[]{:S(2)}, u32[]{:S(2)}) collective-permute-start(f32[1,4096]{1,0:T(1,128)S(1)} %get-tuple-element.19), channel_id=1, source_target_pairs={{0,2},{1,3},{2,0},{3,1},{4,6},{5,7},{6,4},{7,5},{8,10},{9,11},{10,... | collective-permute-start | bytes 49160 | tf_op jit(solution)/shard_map/ppermute | solution.py:48
  27.8 2.3 %collective-permute-start.8 = (f32[1,4096]{1,0:T(1,128)S(1)}, f32[1,4096]{1,0:T(1,128)S(1)}, u32[]{:S(2)}, u32[]{:S(2)}) collective-permute-start(f32[1,4096]{1,0:T(1,128)S(1)} %get-tuple-element.20), channel_id=1, source_target_pairs={{0,1},{1,0},{2,3},{3,2},{4,5},{5,4},{6,7},{7,6},{8,9},{9,8},{10,11... | collective-permute-start | bytes 49160 | tf_op jit(solution)/shard_map/ppermute | solution.py:48

commit v3 on v2

--- a/solution.py
+++ b/solution.py
@@ -32,8 +32,8 @@
 MIB = 1024 * 1024
 VMEM_HELD = 26 * MIB
 PRIORITY = 1
-BLOCK = 512
-AHEAD = 4
+BLOCK = 1024
+TAIL = 128
 
 
 def is_direct(size):
@@ -85,39 +85,43 @@
     return pltpu.with_memory_space_constraint(array, pltpu.HBM)
 
 
-def project_kernel(row_size, block, ahead, hidden, gain, w_query, w_key, w_value, *refs):
+def block_starts(depth):
+    blocks = []
+    start = 0
+    while start < depth:
+        size = min(BLOCK, depth - start)
+        while size > TAIL and size * 2 > depth - start:
+            size //= 2
+        blocks.append((start, size))
+        start += size
+    return blocks
+
+
+def project_kernel(row_size, blocks, hidden, gain, w_query, w_key, w_value, *refs):
     shares = refs[:row_size]
-    inputs_near, gain_near, query_buffer, key_buffer, value_buffer, sems, small, left, total = refs[
+    inputs_near, gain_near, query_buffer, key_buffer, value_buffer, sems, left, total = refs[
         row_size:
     ]
     requests, depth = hidden.shape
     query_width, kv_width = w_query.shape[1], w_key.shape[1]
-    steps = depth // block
-    wide = depth // min(4, steps)
     first = [
-        pltpu.make_async_copy(hidden, inputs_near, small.at[0]),
-        pltpu.make_async_copy(gain, gain_near, small.at[1]),
+        pltpu.make_async_copy(hidden, inputs_near, sems.at[0]),
+        pltpu.make_async_copy(gain, gain_near, sems.at[1]),
     ]
-    stages = []
-    for step in range(steps):
-        start = step * block
-        group = []
-        if start % wide == 0:
-            rows = pl.ds(start, wide)
-            for lane, (far, near) in enumerate(((w_key, key_buffer), (w_value, value_buffer))):
-                copy = pltpu.make_async_copy(
-                    far.at[rows], near.at[rows], sems.at[1 + lane, start // wide]
-                )
-                group.append((copy, 1 + lane, near, start, wide))
-        rows = pl.ds(start, block)
-        copy = pltpu.make_async_copy(w_query.at[rows], query_buffer.at[rows], sems.at[0, step])
-        group.append((copy, 0, query_buffer, start, block))
-        stages.append(group)
+    stages = [
+        (pltpu.make_async_copy(w_key, key_buffer, sems.at[2]), 1, key_buffer, 0, depth),
+        (pltpu.make_async_copy(w_value, value_buffer, sems.at[3]), 2, value_buffer, 0, depth),
+    ]
+    for step, (start, size) in enumerate(blocks):
+        rows = pl.ds(start, size)
+        copy = pltpu.make_async_copy(
+            w_query.at[rows], query_buffer.at[rows], sems.at[4 + step]
+        )
+        stages.append((copy, 0, query_buffer, start, size))
     for copy in first:
         copy.start()
-    for group in stages[:ahead]:
-        for item in group:
-            item[0].start(priority=PRIORITY)
+    for stage in stages:
+        stage[0].start(priority=PRIORITY)
     for copy in first:
         copy.wait()
     inputs = inputs_near[...].astype(jnp.float32)
@@ -125,25 +129,21 @@
     left[:requests, :] = inputs * gain_near[...]
     normed = left[...].astype(jnp.bfloat16)
     squares = jnp.sum(inputs * inputs, axis=1, keepdims=True)
+    total[:requests, query_width + 2 * kv_width :] = jnp.broadcast_to(
+        squares, (requests, HEAD_WIDTH)
+    )
     sums = [None, None, None]
-    for step, group in enumerate(stages):
-        for copy, which, near, start, size in group:
-            copy.wait()
-            if which == 0 and step + ahead < steps:
-                for item in stages[step + ahead]:
-                    item[0].start(priority=PRIORITY)
-            part = jnp.dot(
-                normed[:, start : start + size],
-                near[start : start + size, :],
-                preferred_element_type=jnp.float32,
-            )
-            sums[which] = part if sums[which] is None else sums[which] + part
-    total[:, :query_width] = sums[0]
+    for copy, which, near, start, size in stages:
+        copy.wait()
+        part = jnp.dot(
+            normed[:, start : start + size],
+            near[start : start + size, :],
+            preferred_element_type=jnp.float32,
+        )
+        sums[which] = part if sums[which] is None else sums[which] + part
     total[:, query_width : query_width + kv_width] = sums[1]
     total[:, query_width + kv_width : query_width + 2 * kv_width] = sums[2]
-    total[:requests, query_width + 2 * kv_width :] = jnp.broadcast_to(
-        squares, (requests, HEAD_WIDTH)
-    )
+    total[:, :query_width] = sums[0]
     here = lax.axis_index("row")
     for mask in range(row_size):
         shares[mask][...] = total[pl.ds(here ^ mask, 1), :]
@@ -153,14 +153,13 @@
     row_size = hidden_in.shape[0]
     depth, query_width = w_query.shape
     kv_width = key_weight.shape[1]
-    block = min(depth, BLOCK)
-    steps = depth // block
+    blocks = block_starts(depth)
     width = query_width + 2 * kv_width + HEAD_WIDTH
     near = pl.BlockSpec(memory_space=pltpu.VMEM)
     far = pl.BlockSpec(memory_space=pltpu.HBM)
     size = 2 * depth * (query_width + 2 * kv_width)
     return pl.pallas_call(
-        functools.partial(project_kernel, row_size, block, AHEAD),
+        functools.partial(project_kernel, row_size, blocks),
         out_shape=[jax.ShapeDtypeStruct((1, width), jnp.float32)] * row_size,
         in_specs=[far] * 5,
         out_specs=[near] * row_size,
@@ -170,8 +169,7 @@
             pltpu.VMEM((depth, query_width), jnp.bfloat16),
             pltpu.VMEM((depth, kv_width), jnp.bfloat16),
             pltpu.VMEM((depth, kv_width), jnp.bfloat16),
-            pltpu.SemaphoreType.DMA((3, steps)),
-            pltpu.SemaphoreType.DMA((2,)),
+            pltpu.SemaphoreType.DMA((4 + len(blocks),)),
             pltpu.VMEM((8, depth), jnp.float32),
             pltpu.VMEM((8, width), jnp.float32),
         ],

time: 30.9 us -> 30.2 us (0.977)
  Pallas kernels: 10.4 us -> 9.76 us
    pallas_call x1, Pallas kernels: 7.44 us -> 6.79 us  [project_in(): pl.pallas_call(functools.partial(project_kernel, row_size, blocks), out_s...]
where the time goes in v3:
time: 30.2 us; the launch traced here: 30.1 us
  starting transfers between devices  12.1 us (40%)
  Pallas kernels  9.76 us (32%)
  waiting for transfers between devices  6.58 us (22%)
  other arithmetic  0.89 us (3%)
  between operations  0.7 us (2%)
    ppermute x9, starting transfers between devices, swap_with(): return lax.ppermute(values, axis, [(i, i ^ mask) for i in range(size)])  12.1 us
    pallas_call x1, Pallas kernels, project_in(): pl.pallas_call(functools.partial(project_kernel, row_size, blocks), out_s...  6.79 us
    ppermute x9, waiting for transfers between devices, swap_with(): return lax.ppermute(values, axis, [(i, i ^ mask) for i in range(size)])  6.58 us
    pallas_call x1, Pallas kernels, project_out(): pl.pallas_call(functools.partial(output_kernel, row_size, col_size, min(w...  2.3 us
    pallas_call x1, Pallas kernels, attend(): pl.pallas_call(functools.partial(attend_kernel, row_size), out_shape=jax....  0.67 us
    convert_element_type x1, other arithmetic, direct_body(): return total.astype(jnp.bfloat16)  0.64 us
  transfers between devices with their start and end apart: 9, of which 6 were waited for; matrix products, arithmetic and copies ran while one was open for 1% of the time, Pallas kernels for 0%

profile of v3, /device:TPU:0, one launch (start us, length us, event | category | flops | bytes accessed | tf_op | source)
XLA Modules:
  0.0 30.1 jit_solution(14119860472459208500)
XLA Ops:
  0.0 6.8 %project_in.1 = (f32[1,2432]{1,0:T(1,128)S(1)}, f32[1,2432]{1,0:T(1,128)S(1)}, f32[1,2432]{1,0:T(1,128)S(1)}, f32[1,2432]{1,0:T(1,128)S(1)}) custom-call(bf16[4,4096]{1,0:T(4,128)(2,1)} %hidden.1, f32[1,4096]{1,0:T(1,128)} %bitcast.6, bf16[4096,2048]{1,0:T(8,128)(2,1)} %w_query.1, bf16[4096,128]{1,0:T(8,128)(2,1)} %w_key.1, bf16[4096,128]{1,0:T(8,128)(2,1)} %w_value.1), custom_call_target="tpu_custom_call" | custom-call | flops 75497472 | bytes 18874368 | tf_op jit(solution)/shard_map/project_in/pallas_call | solution.py:161
  6.8 5.1 %collective-permute-start = (f32[1,2432]{1,0:T(1,128)S(1)}, f32[1,2432]{1,0:T(1,128)S(1)}, u32[]{:S(2)}, u32[]{:S(2)}) collective-permute-start(f32[1,2432]{1,0:T(1,128)S(1)} %get-tuple-element.14), channel_id=1, source_target_pairs={{0,12},{4,8},{8,4},{12,0},{1,13},{5,9},{9,5},{13,1},{2,14},{6,10},... | collective-permute-start | bytes 29192 | tf_op jit(solution)/shard_map/ppermute | solution.py:48
  11.9 0.6 %collective-permute-start.2 = (f32[1,2432]{1,0:T(1,128)S(1)}, f32[1,2432]{1,0:T(1,128)S(1)}, u32[]{:S(2)}, u32[]{:S(2)}) collective-permute-start(f32[1,2432]{1,0:T(1,128)S(1)} %get-tuple-element.16), channel_id=1, source_target_pairs={{0,4},{4,0},{8,12},{12,8},{1,5},{5,1},{9,13},{13,9},{2,6},{6,2},{1... | collective-permute-start | bytes 29192 | tf_op jit(solution)/shard_map/ppermute | solution.py:48
  13.2 0.1 fusion.2
  13.3 0.1 fusion
  13.3 0.1 pad_maximum_fusion.refs_5_
  13.4 0.1 pad_maximum_fusion.1.refs_6_
  13.5 0.1 collective-permute-done.refs_1_
  13.6 2.9 %collective-permute-done.1.refs_2_ = f32[1,2432]{1,0:T(1,128)S(1)} collective-permute-done((f32[1,2432]{1,0:T(1,128)S(1)}, f32[1,2432]{1,0:T(1,128)S(1)}, u32[]{:S(2)}, u32[]{:S(2)}) %collective-permute-start.1) | collective-permute-done | bytes 9760 | tf_op jit(solution)/shard_map/ppermute | solution.py:48
  16.5 0.0 collective-permute-done.2.refs_3_
  16.5 0.7 %attend.1.refs_0_ = bf16[16,128]{1,0:T(8,128)(2,1)S(1)} custom-call(f32[1,2432]{1,0:T(1,128)S(1)} %get-tuple-element.13.refs_0_, f32[1,2432]{1,0:T(1,128)S(1)} %collective-permute-done.refs_1_, f32[1,2432]{1,0:T(1,128)S(1)} %collective-permute-done.1.refs_2_, f32[1,2432]{1,0:T(1,128)S(1)} %collective-permute-done.2.refs_3_, s32[1]{0:T(128)S(6)} %copy.10.refs_4_, ...), custom_call_target="tpu_custom_call" | custom-call | flops 16777216 | bytes 1048576 | tf_op jit(solution)/shard_map/attend/pallas_call | solution.py:238
  17.2 1.5 %collective-permute-start.5 = (bf16[16,128]{1,0:T(8,128)(2,1)S(1)}, bf16[16,128]{1,0:T(8,128)(2,1)S(1)}, u32[]{:S(2)}, u32[]{:S(2)}) collective-permute-start(bf16[16,128]{1,0:T(8,128)(2,1)S(1)} %attend.1.refs_0_), channel_id=1, source_target_pairs={{0,12},{4,8},{8,4},{12,0},{1,13},{5,9},{9,5},{13,1},{2,14},{6,10},... | collective-permute-start | bytes 12296 | tf_op jit(solution)/shard_map/ppermute | solution.py:48
  18.7 0.6 %collective-permute-start.4 = (bf16[16,128]{1,0:T(8,128)(2,1)S(1)}, bf16[16,128]{1,0:T(8,128)(2,1)S(1)}, u32[]{:S(2)}, u32[]{:S(2)}) collective-permute-start(bf16[16,128]{1,0:T(8,128)(2,1)S(1)} %attend.1.refs_0_), channel_id=1, source_target_pairs={{0,8},{4,12},{8,0},{12,4},{1,9},{5,13},{9,1},{13,5},{2,10},{6,14},... | collective-permute-start | bytes 12296 | tf_op jit(solution)/shard_map/ppermute | solution.py:48
  19.3 2.3 %collective-permute-start.3 = (bf16[16,128]{1,0:T(8,128)(2,1)S(1)}, bf16[16,128]{1,0:T(8,128)(2,1)S(1)}, u32[]{:S(2)}, u32[]{:S(2)}) collective-permute-start(bf16[16,128]{1,0:T(8,128)(2,1)S(1)} %attend.1.refs_0_), channel_id=1, source_target_pairs={{0,4},{4,0},{8,12},{12,8},{1,5},{5,1},{9,13},{13,9},{2,6},{6,2},{1... | collective-permute-start | bytes 12296 | tf_op jit(solution)/shard_map/ppermute | solution.py:48
  21.6 1.0 %collective-permute-done.5.refs_3_ = bf16[16,128]{1,0:T(8,128)(2,1)S(1)} collective-permute-done((bf16[16,128]{1,0:T(8,128)(2,1)S(1)}, bf16[16,128]{1,0:T(8,128)(2,1)S(1)}, u32[]{:S(2)}, u32[]{:S(2)}) %collective-permute-start.5) | collective-permute-done | bytes 4128 | tf_op jit(solution)/shard_map/ppermute | solution.py:48
  22.6 0.6 %collective-permute-done.4.refs_2_ = bf16[16,128]{1,0:T(8,128)(2,1)S(1)} collective-permute-done((bf16[16,128]{1,0:T(8,128)(2,1)S(1)}, bf16[16,128]{1,0:T(8,128)(2,1)S(1)}, u32[]{:S(2)}, u32[]{:S(2)}) %collective-permute-start.4) | collective-permute-done | bytes 4128 | tf_op jit(solution)/shard_map/ppermute | solution.py:48
  23.2 0.0 collective-permute-done.3.refs_1_
  23.2 2.3 %project_out.1 = (f32[1,4096]{1,0:T(1,128)S(1)}, f32[1,4096]{1,0:T(1,128)S(1)}, f32[1,4096]{1,0:T(1,128)S(1)}, f32[1,4096]{1,0:T(1,128)S(1)}) custom-call(bf16[16,128]{1,0:T(8,128)(2,1)S(1)} %attend.1.refs_0_, bf16[16,128]{1,0:T(8,128)(2,1)S(1)} %collective-permute-done.3.refs_1_, bf16[16,128]{1,0:T(8,128)(2,1)S(1)} %collective-permute-done.4.refs_2_, ...), custom_call_target="tpu_custom_call" | custom-call | flops 67108864 | bytes 16777216 | tf_op jit(solution)/shard_map/project_out/pallas_call | solution.py:281
  25.5 0.1 collective-permute-start.6
  25.6 1.6 %collective-permute-start.7 = (f32[1,4096]{1,0:T(1,128)S(1)}, f32[1,4096]{1,0:T(1,128)S(1)}, u32[]{:S(2)}, u32[]{:S(2)}) collective-permute-start(f32[1,4096]{1,0:T(1,128)S(1)} %get-tuple-element.19), channel_id=1, source_target_pairs={{0,2},{1,3},{2,0},{3,1},{4,6},{5,7},{6,4},{7,5},{8,10},{9,11},{10,... | collective-permute-start | bytes 49160 | tf_op jit(solution)/shard_map/ppermute | solution.py:48
  27.2 0.3 collective-permute-start.8
  27.5 1.4 %collective-permute-done.6 = f32[1,4096]{1,0:T(1,128)S(1)} collective-permute-done((f32[1,4096]{1,0:T(1,128)S(1)}, f32[1,4096]{1,0:T(1,128)S(1)}, u32[]{:S(2)}, u32[]{:S(2)}) %collective-permute-start.6) | collective-permute-done | bytes 16416 | tf_op jit(solution)/shard_map/ppermute | solution.py:48
  28.9 0.5 %collective-permute-done.7 = f32[1,4096]{1,0:T(1,128)S(1)} collective-permute-done((f32[1,4096]{1,0:T(1,128)S(1)}, f32[1,4096]{1,0:T(1,128)S(1)}, u32[]{:S(2)}, u32[]{:S(2)}) %collective-permute-start.7) | collective-permute-done | bytes 16416 | tf_op jit(solution)/shard_map/ppermute | solution.py:48
  29.4 0.6 %add_convert_fusion = bf16[1,4096]{1,0:T(2,128)(2,1)} fusion(f32[1,4096]{1,0:T(1,128)S(1)} %collective-permute-done.8, f32[1,4096]{1,0:T(1,128)S(1)} %collective-permute-done.7, f32[1,4096]{1,0:T(1,128)S(1)} %get-tuple-element.17, f32[1,4096]{1,0:T(1,128)S(1)} %collective-permute-done.6), kind=kLoop, calls=%fused_computation | loop fusion | flops 16384 | bytes 73728 | tf_op jit(solution)/shard_map/convert_element_type | solution.py:410
  (8 shorter events, 0.0 us)
Async XLA Ops:
  0.0 16.5 %copy-start.2 = (bf16[1,2048,128]{2,1,0:T(8,128)(2,1)S(1)}, bf16[1,2048,128]{2,1,0:T(8,128)(2,1)}, u32[]{:S(2)}) copy-start(bf16[1,2048,128]{2,1,0:T(8,128)(2,1)} %param.16) | copy-start | bytes 1572868
  0.0 16.5 %copy-start.1 = (bf16[1,2048,128]{2,1,0:T(8,128)(2,1)S(1)}, bf16[1,2048,128]{2,1,0:T(8,128)(2,1)}, u32[]{:S(2)}) copy-start(bf16[1,2048,128]{2,1,0:T(8,128)(2,1)} %param.15) | copy-start | bytes 1572868
  0.0 23.2 %copy-start = (bf16[2048,4096]{1,0:T(8,128)(2,1)S(1)}, bf16[2048,4096]{1,0:T(8,128)(2,1)}, u32[]{:S(2)}) copy-start(bf16[2048,4096]{1,0:T(8,128)(2,1)} %refs_4_.2) | copy-start | bytes 50331652
  6.8 6.8 %collective-permute-start = (f32[1,2432]{1,0:T(1,128)S(1)}, f32[1,2432]{1,0:T(1,128)S(1)}, u32[]{:S(2)}, u32[]{:S(2)}) collective-permute-start(f32[1,2432]{1,0:T(1,128)S(1)} %get-tuple-element.14), channel_id=1, source_target_pairs={{0,12},{4,8},{8,4},{12,0},{1,13},{5,9},{9,5},{13,1},{2,14},{6,10},... | collective-permute-start | bytes 29192 | tf_op jit(solution)/shard_map/ppermute | solution.py:48
  11.9 4.6 %collective-permute-start.1 = (f32[1,2432]{1,0:T(1,128)S(1)}, f32[1,2432]{1,0:T(1,128)S(1)}, u32[]{:S(2)}, u32[]{:S(2)}) collective-permute-start(f32[1,2432]{1,0:T(1,128)S(1)} %get-tuple-element.15), channel_id=1, source_target_pairs={{0,8},{4,12},{8,0},{12,4},{1,9},{5,13},{9,1},{13,5},{2,10},{6,14},... | collective-permute-start | bytes 29192 | tf_op jit(solution)/shard_map/ppermute | solution.py:48
  11.9 4.6 %collective-permute-start.2 = (f32[1,2432]{1,0:T(1,128)S(1)}, f32[1,2432]{1,0:T(1,128)S(1)}, u32[]{:S(2)}, u32[]{:S(2)}) collective-permute-start(f32[1,2432]{1,0:T(1,128)S(1)} %get-tuple-element.16), channel_id=1, source_target_pairs={{0,4},{4,0},{8,12},{12,8},{1,5},{5,1},{9,13},{13,9},{2,6},{6,2},{1... | collective-permute-start | bytes 29192 | tf_op jit(solution)/shard_map/ppermute | solution.py:48
  17.2 5.5 %collective-permute-start.5 = (bf16[16,128]{1,0:T(8,128)(2,1)S(1)}, bf16[16,128]{1,0:T(8,128)(2,1)S(1)}, u32[]{:S(2)}, u32[]{:S(2)}) collective-permute-start(bf16[16,128]{1,0:T(8,128)(2,1)S(1)} %attend.1.refs_0_), channel_id=1, source_target_pairs={{0,12},{4,8},{8,4},{12,0},{1,13},{5,9},{9,5},{13,1},{2,14},{6,10},... | collective-permute-start | bytes 12296 | tf_op jit(solution)/shard_map/ppermute | solution.py:48
  18.7 4.5 %collective-permute-start.4 = (bf16[16,128]{1,0:T(8,128)(2,1)S(1)}, bf16[16,128]{1,0:T(8,128)(2,1)S(1)}, u32[]{:S(2)}, u32[]{:S(2)}) collective-permute-start(bf16[16,128]{1,0:T(8,128)(2,1)S(1)} %attend.1.refs_0_), channel_id=1, source_target_pairs={{0,8},{4,12},{8,0},{12,4},{1,9},{5,13},{9,1},{13,5},{2,10},{6,14},... | collective-permute-start | bytes 12296 | tf_op jit(solution)/shard_map/ppermute | solution.py:48
  19.3 3.9 %collective-permute-start.3 = (bf16[16,128]{1,0:T(8,128)(2,1)S(1)}, bf16[16,128]{1,0:T(8,128)(2,1)S(1)}, u32[]{:S(2)}, u32[]{:S(2)}) collective-permute-start(bf16[16,128]{1,0:T(8,128)(2,1)S(1)} %attend.1.refs_0_), channel_id=1, source_target_pairs={{0,4},{4,0},{8,12},{12,8},{1,5},{5,1},{9,13},{13,9},{2,6},{6,2},{1... | collective-permute-start | bytes 12296 | tf_op jit(solution)/shard_map/ppermute | solution.py:48
  25.5 3.4 %collective-permute-start.6 = (f32[1,4096]{1,0:T(1,128)S(1)}, f32[1,4096]{1,0:T(1,128)S(1)}, u32[]{:S(2)}, u32[]{:S(2)}) collective-permute-start(f32[1,4096]{1,0:T(1,128)S(1)} %get-tuple-element.18), channel_id=1, source_target_pairs={{0,3},{1,2},{2,1},{3,0},{4,7},{5,6},{6,5},{7,4},{8,11},{9,10},{10,... | collective-permute-start | bytes 49160 | tf_op jit(solution)/shard_map/ppermute | solution.py:48
  25.6 3.8 %collective-permute-start.7 = (f32[1,4096]{1,0:T(1,128)S(1)}, f32[1,4096]{1,0:T(1,128)S(1)}, u32[]{:S(2)}, u32[]{:S(2)}) collective-permute-start(f32[1,4096]{1,0:T(1,128)S(1)} %get-tuple-element.19), channel_id=1, source_target_pairs={{0,2},{1,3},{2,0},{3,1},{4,6},{5,7},{6,4},{7,5},{8,10},{9,11},{10,... | collective-permute-start | bytes 49160 | tf_op jit(solution)/shard_map/ppermute | solution.py:48
  27.2 2.3 %collective-permute-start.8 = (f32[1,4096]{1,0:T(1,128)S(1)}, f32[1,4096]{1,0:T(1,128)S(1)}, u32[]{:S(2)}, u32[]{:S(2)}) collective-permute-start(f32[1,4096]{1,0:T(1,128)S(1)} %get-tuple-element.20), channel_id=1, source_target_pairs={{0,1},{1,0},{2,3},{3,2},{4,5},{5,4},{6,7},{7,6},{8,9},{9,8},{10,11... | collective-permute-start | bytes 49160 | tf_op jit(solution)/shard_map/ppermute | solution.py:48

commit v4 on v3

--- a/solution.py
+++ b/solution.py
@@ -118,6 +118,7 @@
             w_query.at[rows], query_buffer.at[rows], sems.at[4 + step]
         )
         stages.append((copy, 0, query_buffer, start, size))
+    stages = stages[2:4] + stages[:2] + stages[4:]
     for copy in first:
         copy.start()
     for stage in stages:
@@ -181,6 +182,25 @@
     )(*map(in_hbm, (hidden_in, norm_gain.reshape(1, depth), w_query, key_weight, value_weight)))
 
 
+def turn_kernel(ready, keys, turned):
+    turned[...] = keys[...].T
+
+
+def turn_keys(ready, keys):
+    near = pl.BlockSpec(memory_space=pltpu.VMEM)
+    return pl.pallas_call(
+        turn_kernel,
+        out_shape=jax.ShapeDtypeStruct(keys.shape[::-1], keys.dtype),
+        in_specs=[near, near],
+        out_specs=near,
+        compiler_params=pltpu.CompilerParams(vmem_limit_bytes=4 * MIB),
+        cost_estimate=pl.CostEstimate(
+            flops=0, bytes_accessed=4 * keys.shape[0] * keys.shape[1], transcendentals=0
+        ),
+        name="turn_keys",
+    )(ready, keys)
+
+
 def attend_kernel(row_size, *refs):
     shares = refs[:row_size]
     length, cosine, sine, keys, values, heads, rows = refs[row_size:]
@@ -204,10 +224,7 @@
     value_new = value_row.astype(jnp.bfloat16).astype(jnp.float32)
     inverse = 1.0 / width**0.5
     scores = (
-        lax.dot_general(
-            query, keys[...], (((1,), (1,)), ((), ())), preferred_element_type=jnp.float32
-        )
-        * inverse
+        jnp.dot(query, keys[...], preferred_element_type=jnp.float32) * inverse
     )
     score_new = (
         jnp.sum(query.astype(jnp.float32) * key_new, axis=1, keepdims=True) * inverse
@@ -227,7 +244,7 @@
 
 def attend(shares, lengths, keys, values, heads_count):
     row_size = len(shares)
-    slots, width = keys.shape
+    width, slots = keys.shape
     half = width // 2
     frequency = 500000.0 ** (-(jnp.arange(half, dtype=jnp.float32) * 2.0 / width))
     angles = lengths.astype(jnp.float32)[:, None] * frequency[None, :]
@@ -271,7 +288,10 @@
     here = lax.axis_index("row")
     lane = lax.axis_index("col")
     for mask in range(col_size):
-        shares[mask][...] = total[pl.ds((lane ^ mask) ^ here, 1), :]
+        row = total[pl.ds((lane ^ mask) ^ here, 1), :]
+        piece = shares[mask].shape[1]
+        for part in range(8):
+            shares[mask][part : part + 1, :] = row[:, part * piece : (part + 1) * piece]
 
 
 def project_out(blocks, w_output, col_size):
@@ -280,7 +300,7 @@
     whole = pl.BlockSpec(memory_space=pltpu.VMEM)
     return pl.pallas_call(
         functools.partial(output_kernel, row_size, col_size, min(width, 512)),
-        out_shape=[jax.ShapeDtypeStruct((1, width), jnp.float32)] * col_size,
+        out_shape=[jax.ShapeDtypeStruct((8, width // 8), jnp.float32)] * col_size,
         in_specs=[whole] * (row_size + 1),
         out_specs=[whole] * col_size,
         scratch_shapes=[
@@ -293,6 +313,30 @@
         ),
         name="project_out",
     )(*blocks, w_output)
+
+
+def sum_kernel(*refs):
+    parts = refs[:-1]
+    total = parts[0][...]
+    for part in parts[1:]:
+        total = total + part[...]
+    piece = total.shape[1]
+    for part in range(8):
+        refs[-1][:, part * piece : (part + 1) * piece] = total[part : part + 1, :].astype(
+            refs[-1].dtype
+        )
+
+
+def sum_rows(parts):
+    near = pl.BlockSpec(memory_space=pltpu.VMEM)
+    return pl.pallas_call(
+        sum_kernel,
+        out_shape=jax.ShapeDtypeStruct((1, parts[0].size), jnp.bfloat16),
+        in_specs=[near] * len(parts),
+        out_specs=near,
+        compiler_params=pltpu.CompilerParams(vmem_limit_bytes=4 * MIB),
+        name="sum_rows",
+    )(*parts)
 
 
 def body(
@@ -396,18 +440,14 @@
     shares = [parts[0]] + [
         swap_with(parts[mask], "row", size, mask) for mask in partner_order(size)
     ]
-    mine = attend(
-        shares, lengths, stored_keys[0], stored_values[0], w_query.shape[1] // head_size
-    )
+    keys = turn_keys(parts[0], stored_keys[0])
+    mine = attend(shares, lengths, keys, stored_values[0], w_query.shape[1] // head_size)
     blocks = [mine] + [None] * (size - 1)
     for mask in partner_order(size):
         blocks[mask] = swap_with(mine, "row", size, mask)
     parts = project_out(blocks, w_output, size)
     received = [swap_with(parts[mask], "col", size, mask) for mask in partner_order(size)]
-    total = parts[0]
-    for part in received:
-        total = total + part
-    return total.astype(jnp.bfloat16)
+    return sum_rows([parts[0]] + received)
 
 
 def fits_direct(mesh):

time: 30.2 us -> 30.2 us (level)
  Pallas kernels: 9.76 us -> 10.5 us
  other arithmetic: 0.89 us -> 0.25 us
    pallas_call x0 -> x2, Pallas kernels: none -> 0.81 us  [the longest x1 0.62 us: sum_rows(): pl.pallas_call(sum_kernel, out_shape=jax.ShapeDtypeStruct((1, parts[0].si...]
    convert_element_type x1 -> x0, other arithmetic: 0.64 us -> none  [direct_body(): return total.astype(jnp.bfloat16)]
  transfers between devices with their start and end apart: 9 -> 9, of which waited for: 6 -> 5; matrix products, arithmetic and copies ran while one was open for 1% -> 1% of each run, Pallas kernels for 0% -> 1%
where the time goes in v4:
time: 30.2 us; the launch traced here: 30 us
  starting transfers between devices  12.1 us (40%)
  Pallas kernels  10.5 us (35%)
  waiting for transfers between devices  6.38 us (21%)
  between operations  0.71 us (2%)
    ppermute x9, starting transfers between devices, swap_with(): return lax.ppermute(values, axis, [(i, i ^ mask) for i in range(size)])  12.1 us
    pallas_call x1, Pallas kernels, project_in(): pl.pallas_call(functools.partial(project_kernel, row_size, blocks), out_s...  6.8 us
    ppermute x9, waiting for transfers between devices, swap_with(): return lax.ppermute(values, axis, [(i, i ^ mask) for i in range(size)])  6.38 us
    pallas_call x1, Pallas kernels, project_out(): pl.pallas_call(functools.partial(output_kernel, row_size, col_size, min(w...  2.31 us
    pallas_call x1, Pallas kernels, sum_rows(): pl.pallas_call(sum_kernel, out_shape=jax.ShapeDtypeStruct((1, parts[0].si...  0.62 us
    pallas_call x1, Pallas kernels, attend(): pl.pallas_call(functools.partial(attend_kernel, row_size), out_shape=jax....  0.62 us
  transfers between devices with their start and end apart: 9, of which 5 were waited for; matrix products, arithmetic and copies ran while one was open for 1% of the time, Pallas kernels for 1%

profile of v4, /device:TPU:0, one launch (start us, length us, event | category | flops | bytes accessed | tf_op | source)
XLA Modules:
  0.0 30.0 jit_solution(9647354467962441980)
XLA Ops:
  0.0 6.8 %project_in.1 = (f32[1,2432]{1,0:T(1,128)S(1)}, f32[1,2432]{1,0:T(1,128)S(1)}, f32[1,2432]{1,0:T(1,128)S(1)}, f32[1,2432]{1,0:T(1,128)S(1)}) custom-call(bf16[4,4096]{1,0:T(4,128)(2,1)} %hidden.1, f32[1,4096]{1,0:T(1,128)} %bitcast.6, bf16[4096,2048]{1,0:T(8,128)(2,1)} %w_query.1, bf16[4096,128]{1,0:T(8,128)(2,1)} %w_key.1, bf16[4096,128]{1,0:T(8,128)(2,1)} %w_value.1), custom_call_target="tpu_custom_call" | custom-call | flops 75497472 | bytes 18874368 | tf_op jit(solution)/shard_map/project_in/pallas_call | solution.py:162
  6.8 5.1 %collective-permute-start = (f32[1,2432]{1,0:T(1,128)S(1)}, f32[1,2432]{1,0:T(1,128)S(1)}, u32[]{:S(2)}, u32[]{:S(2)}) collective-permute-start(f32[1,2432]{1,0:T(1,128)S(1)} %get-tuple-element.14), channel_id=1, source_target_pairs={{0,12},{4,8},{8,4},{12,0},{1,13},{5,9},{9,5},{13,1},{2,14},{6,10},... | collective-permute-start | bytes 29192 | tf_op jit(solution)/shard_map/ppermute | solution.py:48
  11.9 0.0 collective-permute-start.1
  11.9 0.6 %collective-permute-start.2 = (f32[1,2432]{1,0:T(1,128)S(1)}, f32[1,2432]{1,0:T(1,128)S(1)}, u32[]{:S(2)}, u32[]{:S(2)}) collective-permute-start(f32[1,2432]{1,0:T(1,128)S(1)} %get-tuple-element.16), channel_id=1, source_target_pairs={{0,4},{4,0},{8,12},{12,8},{1,5},{5,1},{9,13},{13,9},{2,6},{6,2},{1... | collective-permute-start | bytes 29192 | tf_op jit(solution)/shard_map/ppermute | solution.py:48
  13.2 0.1 fusion.2
  13.3 0.1 fusion
  13.3 0.1 pad_maximum_fusion.refs_5_
  13.4 0.1 pad_maximum_fusion.1.refs_6_
  13.5 0.2 turn_keys.1.refs_7_
  13.7 2.8 %collective-permute-done.1.refs_2_ = f32[1,2432]{1,0:T(1,128)S(1)} collective-permute-done((f32[1,2432]{1,0:T(1,128)S(1)}, f32[1,2432]{1,0:T(1,128)S(1)}, u32[]{:S(2)}, u32[]{:S(2)}) %collective-permute-start.1) | collective-permute-done | bytes 9760 | tf_op jit(solution)/shard_map/ppermute | solution.py:48
  16.5 0.6 %attend.1.refs_0_ = bf16[16,128]{1,0:T(8,128)(2,1)S(1)} custom-call(f32[1,2432]{1,0:T(1,128)S(1)} %get-tuple-element.13.ready.refs_0_, f32[1,2432]{1,0:T(1,128)S(1)} %collective-permute-done.refs_1_, f32[1,2432]{1,0:T(1,128)S(1)} %collective-permute-done.1.refs_2_, f32[1,2432]{1,0:T(1,128)S(1)} %collective-permute-done.2.refs_3_, s32[1]{0:T(128)S(6)} %copy.10.refs_4_, ...), custom_call_target="tpu_custom_call" | custom-call | flops 16777216 | bytes 1048576 | tf_op jit(solution)/shard_map/attend/pallas_call | solution.py:255
  17.1 1.5 %collective-permute-start.5 = (bf16[16,128]{1,0:T(8,128)(2,1)S(1)}, bf16[16,128]{1,0:T(8,128)(2,1)S(1)}, u32[]{:S(2)}, u32[]{:S(2)}) collective-permute-start(bf16[16,128]{1,0:T(8,128)(2,1)S(1)} %attend.1.refs_0_), channel_id=1, source_target_pairs={{0,12},{4,8},{8,4},{12,0},{1,13},{5,9},{9,5},{13,1},{2,14},{6,10},... | collective-permute-start | bytes 12296 | tf_op jit(solution)/shard_map/ppermute | solution.py:48
  18.6 0.6 %collective-permute-start.4 = (bf16[16,128]{1,0:T(8,128)(2,1)S(1)}, bf16[16,128]{1,0:T(8,128)(2,1)S(1)}, u32[]{:S(2)}, u32[]{:S(2)}) collective-permute-start(bf16[16,128]{1,0:T(8,128)(2,1)S(1)} %attend.1.refs_0_), channel_id=1, source_target_pairs={{0,8},{4,12},{8,0},{12,4},{1,9},{5,13},{9,1},{13,5},{2,10},{6,14},... | collective-permute-start | bytes 12296 | tf_op jit(solution)/shard_map/ppermute | solution.py:48
  19.3 2.3 %collective-permute-start.3 = (bf16[16,128]{1,0:T(8,128)(2,1)S(1)}, bf16[16,128]{1,0:T(8,128)(2,1)S(1)}, u32[]{:S(2)}, u32[]{:S(2)}) collective-permute-start(bf16[16,128]{1,0:T(8,128)(2,1)S(1)} %attend.1.refs_0_), channel_id=1, source_target_pairs={{0,4},{4,0},{8,12},{12,8},{1,5},{5,1},{9,13},{13,9},{2,6},{6,2},{1... | collective-permute-start | bytes 12296 | tf_op jit(solution)/shard_map/ppermute | solution.py:48
  21.6 1.0 %collective-permute-done.5.refs_3_ = bf16[16,128]{1,0:T(8,128)(2,1)S(1)} collective-permute-done((bf16[16,128]{1,0:T(8,128)(2,1)S(1)}, bf16[16,128]{1,0:T(8,128)(2,1)S(1)}, u32[]{:S(2)}, u32[]{:S(2)}) %collective-permute-start.5) | collective-permute-done | bytes 4128 | tf_op jit(solution)/shard_map/ppermute | solution.py:48
  22.6 0.6 %collective-permute-done.4.refs_2_ = bf16[16,128]{1,0:T(8,128)(2,1)S(1)} collective-permute-done((bf16[16,128]{1,0:T(8,128)(2,1)S(1)}, bf16[16,128]{1,0:T(8,128)(2,1)S(1)}, u32[]{:S(2)}, u32[]{:S(2)}) %collective-permute-start.4) | collective-permute-done | bytes 4128 | tf_op jit(solution)/shard_map/ppermute | solution.py:48
  23.2 0.0 collective-permute-done.3.refs_1_
  23.2 2.3 %project_out.1 = (f32[8,512]{1,0:T(8,128)S(1)}, f32[8,512]{1,0:T(8,128)S(1)}, f32[8,512]{1,0:T(8,128)S(1)}, f32[8,512]{1,0:T(8,128)S(1)}) custom-call(bf16[16,128]{1,0:T(8,128)(2,1)S(1)} %attend.1.refs_0_, bf16[16,128]{1,0:T(8,128)(2,1)S(1)} %collective-permute-done.3.refs_1_, bf16[16,128]{1,0:T(8,128)(2,1)S(1)} %collective-permute-done.4.refs_2_, ...), custom_call_target="tpu_custom_call" | custom-call | flops 67108864 | bytes 16777216 | tf_op jit(solution)/shard_map/project_out/pallas_call | solution.py:301
  25.5 0.1 collective-permute-start.6
  25.6 1.6 %collective-permute-start.7 = (f32[8,512]{1,0:T(8,128)S(1)}, f32[8,512]{1,0:T(8,128)S(1)}, u32[]{:S(2)}, u32[]{:S(2)}) collective-permute-start(f32[8,512]{1,0:T(8,128)S(1)} %get-tuple-element.19), channel_id=1, source_target_pairs={{0,2},{1,3},{2,0},{3,1},{4,6},{5,7},{6,4},{7,5},{8,10},{9,11},{10,... | collective-permute-start | bytes 49160 | tf_op jit(solution)/shard_map/ppermute | solution.py:48
  27.1 0.3 collective-permute-start.8
  27.4 1.4 %collective-permute-done.6.refs_1_ = f32[8,512]{1,0:T(8,128)S(1)} collective-permute-done((f32[8,512]{1,0:T(8,128)S(1)}, f32[8,512]{1,0:T(8,128)S(1)}, u32[]{:S(2)}, u32[]{:S(2)}) %collective-permute-start.6) | collective-permute-done | bytes 16416 | tf_op jit(solution)/shard_map/ppermute | solution.py:48
  28.9 0.5 %collective-permute-done.7.refs_2_ = f32[8,512]{1,0:T(8,128)S(1)} collective-permute-done((f32[8,512]{1,0:T(8,128)S(1)}, f32[8,512]{1,0:T(8,128)S(1)}, u32[]{:S(2)}, u32[]{:S(2)}) %collective-permute-start.7) | collective-permute-done | bytes 16416 | tf_op jit(solution)/shard_map/ppermute | solution.py:48
  29.4 0.6 %sum_rows.1 = bf16[1,4096]{1,0:T(2,128)(2,1)} custom-call(f32[8,512]{1,0:T(8,128)S(1)} %get-tuple-element.17.refs_0_, f32[8,512]{1,0:T(8,128)S(1)} %collective-permute-done.6.refs_1_, f32[8,512]{1,0:T(8,128)S(1)} %collective-permute-done.7.refs_2_, f32[8,512]{1,0:T(8,128)S(1)} %collective-permute-done.8.refs_3_), custom_call_target="tpu_custom_call" | custom-call | tf_op jit(solution)/shard_map/sum_rows/pallas_call | solution.py:332
  (9 shorter events, 0.0 us)
Async XLA Ops:
  0.0 13.5 %copy-start.2 = (bf16[1,2048,128]{2,1,0:T(8,128)(2,1)S(1)}, bf16[1,2048,128]{2,1,0:T(8,128)(2,1)}, u32[]{:S(2)}) copy-start(bf16[1,2048,128]{2,1,0:T(8,128)(2,1)} %param.15) | copy-start | bytes 1572868
  0.0 16.5 %copy-start.1 = (bf16[1,2048,128]{2,1,0:T(8,128)(2,1)S(1)}, bf16[1,2048,128]{2,1,0:T(8,128)(2,1)}, u32[]{:S(2)}) copy-start(bf16[1,2048,128]{2,1,0:T(8,128)(2,1)} %param.16) | copy-start | bytes 1572868
  0.0 23.2 %copy-start = (bf16[2048,4096]{1,0:T(8,128)(2,1)S(1)}, bf16[2048,4096]{1,0:T(8,128)(2,1)}, u32[]{:S(2)}) copy-start(bf16[2048,4096]{1,0:T(8,128)(2,1)} %refs_4_.2) | copy-start | bytes 50331652
  6.8 6.9 %collective-permute-start = (f32[1,2432]{1,0:T(1,128)S(1)}, f32[1,2432]{1,0:T(1,128)S(1)}, u32[]{:S(2)}, u32[]{:S(2)}) collective-permute-start(f32[1,2432]{1,0:T(1,128)S(1)} %get-tuple-element.14), channel_id=1, source_target_pairs={{0,12},{4,8},{8,4},{12,0},{1,13},{5,9},{9,5},{13,1},{2,14},{6,10},... | collective-permute-start | bytes 29192 | tf_op jit(solution)/shard_map/ppermute | solution.py:48
  11.9 4.6 %collective-permute-start.1 = (f32[1,2432]{1,0:T(1,128)S(1)}, f32[1,2432]{1,0:T(1,128)S(1)}, u32[]{:S(2)}, u32[]{:S(2)}) collective-permute-start(f32[1,2432]{1,0:T(1,128)S(1)} %get-tuple-element.15), channel_id=1, source_target_pairs={{0,8},{4,12},{8,0},{12,4},{1,9},{5,13},{9,1},{13,5},{2,10},{6,14},... | collective-permute-start | bytes 29192 | tf_op jit(solution)/shard_map/ppermute | solution.py:48
  11.9 4.6 %collective-permute-start.2 = (f32[1,2432]{1,0:T(1,128)S(1)}, f32[1,2432]{1,0:T(1,128)S(1)}, u32[]{:S(2)}, u32[]{:S(2)}) collective-permute-start(f32[1,2432]{1,0:T(1,128)S(1)} %get-tuple-element.16), channel_id=1, source_target_pairs={{0,4},{4,0},{8,12},{12,8},{1,5},{5,1},{9,13},{13,9},{2,6},{6,2},{1... | collective-permute-start | bytes 29192 | tf_op jit(solution)/shard_map/ppermute | solution.py:48
  17.1 5.5 %collective-permute-start.5 = (bf16[16,128]{1,0:T(8,128)(2,1)S(1)}, bf16[16,128]{1,0:T(8,128)(2,1)S(1)}, u32[]{:S(2)}, u32[]{:S(2)}) collective-permute-start(bf16[16,128]{1,0:T(8,128)(2,1)S(1)} %attend.1.refs_0_), channel_id=1, source_target_pairs={{0,12},{4,8},{8,4},{12,0},{1,13},{5,9},{9,5},{13,1},{2,14},{6,10},... | collective-permute-start | bytes 12296 | tf_op jit(solution)/shard_map/ppermute | solution.py:48
  18.6 4.5 %collective-permute-start.4 = (bf16[16,128]{1,0:T(8,128)(2,1)S(1)}, bf16[16,128]{1,0:T(8,128)(2,1)S(1)}, u32[]{:S(2)}, u32[]{:S(2)}) collective-permute-start(bf16[16,128]{1,0:T(8,128)(2,1)S(1)} %attend.1.refs_0_), channel_id=1, source_target_pairs={{0,8},{4,12},{8,0},{12,4},{1,9},{5,13},{9,1},{13,5},{2,10},{6,14},... | collective-permute-start | bytes 12296 | tf_op jit(solution)/shard_map/ppermute | solution.py:48
  19.3 3.9 %collective-permute-start.3 = (bf16[16,128]{1,0:T(8,128)(2,1)S(1)}, bf16[16,128]{1,0:T(8,128)(2,1)S(1)}, u32[]{:S(2)}, u32[]{:S(2)}) collective-permute-start(bf16[16,128]{1,0:T(8,128)(2,1)S(1)} %attend.1.refs_0_), channel_id=1, source_target_pairs={{0,4},{4,0},{8,12},{12,8},{1,5},{5,1},{9,13},{13,9},{2,6},{6,2},{1... | collective-permute-start | bytes 12296 | tf_op jit(solution)/shard_map/ppermute | solution.py:48
  25.5 3.4 %collective-permute-start.6 = (f32[8,512]{1,0:T(8,128)S(1)}, f32[8,512]{1,0:T(8,128)S(1)}, u32[]{:S(2)}, u32[]{:S(2)}) collective-permute-start(f32[8,512]{1,0:T(8,128)S(1)} %get-tuple-element.18), channel_id=1, source_target_pairs={{0,3},{1,2},{2,1},{3,0},{4,7},{5,6},{6,5},{7,4},{8,11},{9,10},{10,... | collective-permute-start | bytes 49160 | tf_op jit(solution)/shard_map/ppermute | solution.py:48
  25.6 3.8 %collective-permute-start.7 = (f32[8,512]{1,0:T(8,128)S(1)}, f32[8,512]{1,0:T(8,128)S(1)}, u32[]{:S(2)}, u32[]{:S(2)}) collective-permute-start(f32[8,512]{1,0:T(8,128)S(1)} %get-tuple-element.19), channel_id=1, source_target_pairs={{0,2},{1,3},{2,0},{3,1},{4,6},{5,7},{6,4},{7,5},{8,10},{9,11},{10,... | collective-permute-start | bytes 49160 | tf_op jit(solution)/shard_map/ppermute | solution.py:48
  27.1 2.3 %collective-permute-start.8 = (f32[8,512]{1,0:T(8,128)S(1)}, f32[8,512]{1,0:T(8,128)S(1)}, u32[]{:S(2)}, u32[]{:S(2)}) collective-permute-start(f32[8,512]{1,0:T(8,128)S(1)} %get-tuple-element.20), channel_id=1, source_target_pairs={{0,1},{1,0},{2,3},{3,2},{4,5},{5,4},{6,7},{7,6},{8,9},{9,8},{10,11... | collective-permute-start | bytes 49160 | tf_op jit(solution)/shard_map/ppermute | solution.py:48
